TPU v7x, 32 devices: a whole 2x2x4 slice. The times are simulated.
32 devices in a mesh: loop: 16 (over z, x, core), rep: 2 (over y).
Axes of the slice: x: 2, y: 2, z: 4, core: 2. Of those that a mesh axis runs over, the one named last changes fastest.
Arguments:
- queries: bfloat16 [8192, 4096], P(('loop', 'rep')), may hold values from -2.5 to 2.5
- passages: bfloat16 [128, 4096], P('loop'), may hold values from -0.6 to 0.6
- index_rows: bfloat16 [8192, 4096], P(('loop', 'rep')), may hold values from -0.7 to 0.7
- positive: int32 [8192], P(('loop', 'rep')), may hold values from 0 to 127, as said below
- hard_rows: int32 [16, 32, 8], P('loop'), may hold values from 0 to 255
- hard_counts: int32 [16, 32], P('loop'), may hold values from 0 to 8, as said below
Outputs:
- query_grad: float32 [8192, 4096], P(('loop', 'rep'))
- passage_grad: float32 [128, 4096], P('loop')
- mean_loss: float32 [], replicated
Inputs may be any that keep to these rules, and one draw needn't show every extreme that they name: `hard_counts`: in every draw some index shard takes 8 live slots from every query block. Every passage is the positive of exactly 64 queries.
All inputs are finite; a program needn't handle non-finite values.
Results may differ from a plain program's by a relative error of at most 0.0015.
Values may be sent and summed in bfloat16 or wider, within the bound.
No kernel may reach another device: no remote copies, remote signals or barrier semaphores. Data moves between devices by JAX's collectives and lax.ppermute only.
A program may use at most 128 MiB of HBM per device.

v0:
```python
import functools

import jax
import jax.numpy as jnp
from jax import lax
from jax.experimental import pallas as pl
from jax.experimental.pallas import tpu as pltpu
from jax.sharding import PartitionSpec as P


def budget(*arrays):
    total = sum(a.size * a.dtype.itemsize for a in arrays)
    return pltpu.CompilerParams(vmem_limit_bytes=total + total // 4 + 6 * 1024 * 1024)


WHOLE = pl.BlockSpec(memory_space=pltpu.VMEM)
SCALARS = pl.BlockSpec(memory_space=pltpu.SMEM)
LOSS = 128


def exchange(value, axes, mask):
    size = 1
    for axis in axes:
        size *= lax.axis_size(axis)
    return lax.ppermute(value, axes, [(i, i ^ mask) for i in range(size)])


def pick_rows(count, reach, meta, other, own, after, *refs):
    asked, (plane, *pieces) = refs[:reach], refs[reach:]
    me, rep = meta[0], meta[1]
    owners = asked[0].shape[1]
    slots = plane.shape[0] // (2 * count)
    lanes = lax.broadcasted_iota(jnp.int32, (slots, owners), 1)
    rows = lax.broadcasted_iota(jnp.int32, (slots, own.shape[0]), 1)

    def hot(owner):
        picked = []
        for m in range(count + len(pieces)):
            at = m % 2 * slots
            tile = asked[m // 2][at:at + slots, :]
            column = jnp.sum(jnp.where(lanes == owner, tile, 0), axis=1, keepdims=True)
            picked.append(jnp.where(column == rows, 1.0, 0.0))
        return jnp.concatenate(picked, axis=0).astype(jnp.bfloat16)

    hot_own = hot(me * 2 + rep)
    hot_other = hot((me ^ 1) * 2 + rep)
    got_other = jnp.dot(hot_other, other[...], preferred_element_type=jnp.float32)
    got_own = jnp.dot(hot_own, own[...], preferred_element_type=jnp.float32)
    for m in range(count + len(pieces)):
        part = slice(m * slots, (m + 1) * slots)
        value = jnp.concatenate([got_own[part], got_other[part]], axis=0).astype(jnp.bfloat16)
        if m < count:
            plane[m * 2 * slots:(m + 1) * 2 * slots, :] = value
        else:
            pieces[m - count][...] = value


def pack_kernel(layouts, *refs):
    ins, outs = refs[:-len(layouts)], refs[-len(layouts):]
    for layout, out in zip(layouts, outs):
        at = 0
        for which, first, rows in layout:
            out[at:at + rows, :] = ins[which][first:first + rows, :]
            at += rows


def pack(layouts, *arrays):
    shapes = [
        jax.ShapeDtypeStruct((sum(rows for _, _, rows in layout), arrays[0].shape[1]), arrays[0].dtype)
        for layout in layouts
    ]
    size = sum(shape.size for shape in shapes)
    return pl.pallas_call(
        functools.partial(pack_kernel, layouts),
        out_shape=shapes,
        in_specs=[WHOLE] * len(arrays),
        out_specs=[WHOLE] * len(layouts),
        compiler_params=budget(*shapes, *arrays),
        cost_estimate=pl.CostEstimate(flops=size, bytes_accessed=4 * size, transcendentals=0),
    )(*arrays)


def stack(counts, refs, out):
    at = 0
    for rows, ref in zip(counts, refs):
        out[at:at + rows, :] = ref[:rows, :]
        at += rows


def scored(queries, rows):
    return 50.0 * lax.dot_general(
        queries[...], rows[...], (((1,), (1,)), ((), ())), preferred_element_type=jnp.float32
    )


def early_kernel(counts, queries, *refs):
    *batches, scores_out, rows = refs
    stack(counts, batches, rows)
    scores_out[...] = scored(queries, rows)


def lookup(index, values):
    total = jnp.zeros_like(index)
    for i, value in enumerate(values):
        total = jnp.where(index == i, value, total)
    return total


def score_kernel(
    counts, passages, columns, slots, meta, hard_counts, queries, positive, scores_ref, *refs
):
    *batches, out_1, out_2, rows, send_out = refs
    batches = batches[-passages:] + batches[:-passages]
    me, rep = meta[0], meta[1]
    stack(counts, batches, rows)
    side = send_out.shape[0]
    block = side // len(columns[0][0])
    blocks = [scores_ref[...], scored(queries, rows)]
    wanted = jnp.broadcast_to(positive[...].astype(jnp.float32), (8, positive.shape[1]))
    wanted = jnp.transpose(wanted)[:, :1]
    onehots = []
    for i, (order, places) in enumerate(columns):
        lane = lax.broadcasted_iota(jnp.int32, (1, blocks[i].shape[1]), 1)
        passage = lane < side
        ids = (lookup(lane // block, order) * block + lane % block) ^ (me * block)
        spot = jnp.where(passage, 0, lane - side)
        owner = lookup(spot // (2 * slots), [4 * m + p for m, p in places])
        owner = (owner + spot // slots % 2 * 2) ^ (me * 2 + rep)
        taken = lookup(owner, [hard_counts[0, o] for o in range(hard_counts.shape[1])])
        live = passage | (spot % slots < taken)
        onehots.append(
            jnp.where((wanted == ids.astype(jnp.float32)) & passage, 1.0, 0.0)
        )
        blocks[i] = jnp.where(live, blocks[i], -jnp.inf)
    tops = [jnp.max(value, axis=1, keepdims=True) for value in blocks]
    row_top = jnp.maximum(tops[0], tops[1])
    sums = [jnp.sum(jnp.exp(value - row_top), axis=1, keepdims=True) for value in blocks]
    log_total = row_top + jnp.log(sums[0] + sums[1])
    weights = [
        (jnp.exp(value - log_total) - onehot).astype(jnp.bfloat16)
        for value, onehot in zip(blocks, onehots)
    ]
    hit = sum(
        jnp.sum(jnp.where(onehot > 0, value, 0.0), axis=1, keepdims=True)
        for value, onehot in zip(blocks, onehots)
    )
    project(send_out, weights[1][:, :side], queries, meta[1], jnp.sum(log_total - hit))
    out_1[...] = weights[0]
    out_2[...] = weights[1]


def project(out, weights, queries, rep, loss):
    half = queries.shape[1] // 2
    for i, side in enumerate((rep, 1 - rep)):
        product = lax.dot_general(
            weights, queries[:, pl.ds(pl.multiple_of(side * half, half), half)],
            (((0,), (0,)), ((), ())), preferred_element_type=jnp.float32,
        )
        at = i * (half + LOSS)
        out[:, at:at + half] = 50.0 * product
        out[:, at + half:at + half + LOSS] = jnp.full((out.shape[0], LOSS), loss, jnp.float32)


def keep_kernel(meta, weights, queries, send, out):
    half = queries.shape[1] // 2
    project(
        out, weights[:, :out.shape[0]], queries, meta[1], send[0:1, half:half + 1]
    )


def first_sum(kept, sent, own, to_x, to_y, to_xy):
    rows, columns = own.shape
    half = columns - LOSS
    lanes = lax.broadcasted_iota(jnp.int32, (rows, LOSS), 1)
    for out, down, across in ((own, 0, 0), (to_x, 1, 0), (to_y, 0, 1), (to_xy, 1, 1)):
        at = pl.ds(down * rows, rows)
        data = pl.ds(across * columns, half)
        out[:, :half] = (kept[at, data] + sent[at, data]).astype(out.dtype)
        tile = pl.ds(across * columns + half, LOSS)
        loss = kept[at, tile] + sent[at, tile]
        high = loss.astype(jnp.bfloat16).astype(jnp.float32)
        out[:, half:] = jnp.where(lanes < LOSS // 2, high, loss - high).astype(out.dtype)


def second_sum(own, from_x, from_y, from_xy, after, *outs):
    rows = outs[0].shape[0]
    for i, out in enumerate(outs):
        at = pl.ds(i * rows, rows)
        out[...] = (own[at] + from_x[at].astype(jnp.float32)) + (
            from_y[at].astype(jnp.float32) + from_xy[at].astype(jnp.float32)
        )


def grad_kernel(weights_1, weights_2, rows_1, rows_2, out, done):
    done[...] = jnp.zeros(done.shape, done.dtype)
    out[...] = 50.0 * (
        jnp.dot(weights_1[...], rows_1[...], preferred_element_type=jnp.float32)
        + jnp.dot(weights_2[...], rows_2[...], preferred_element_type=jnp.float32)
    )


def shards(queries, passages, index_rows, positive, hard_rows, hard_counts):
    loop = lax.axis_size("loop")
    reps = lax.axis_size("rep")
    me = lax.axis_index("loop").astype(jnp.int32)
    rep = lax.axis_index("rep").astype(jnp.int32)
    count, width = queries.shape
    block = passages.shape[0]
    owners, slots = hard_rows.shape[1:]
    half = width // 2
    chips = loop // 2
    meta = jnp.stack([me, rep])
    both = ("loop", "rep")

    other_rows = exchange(index_rows, ("loop",), 1)
    rest = loop // 4
    wanted = jnp.transpose(hard_rows, (0, 2, 1)).reshape(slots, owners)
    asked, = pack([[(0, 0, slots), (1, 0, slots)]], wanted, exchange(wanted, ("loop",), 2))
    asked = [asked] + [exchange(asked, ("loop",), 4 * k) for k in range(1, rest)]
    own_rows, = pack([[(0, 0, index_rows.shape[0])]], index_rows)

    bits = [loop // 2 >> i for i in range(loop.bit_length() - 4)] + [4, 2, 1]
    orders = [0]
    for bit in bits:
        orders = orders + [o | bit for o in orders]
    for bit in bits[:-4]:
        passages = jnp.concatenate([passages, exchange(passages, ("loop",), bit)], axis=0)
    passages_z = exchange(passages, ("loop",), bits[-4])

    depth = 2 * slots
    have = 2 * passages.shape[0]
    top = chips // 2
    outs = [jax.ShapeDtypeStruct((top * depth, width), jnp.bfloat16)]
    outs += [jax.ShapeDtypeStruct((depth, width), jnp.bfloat16)] * top
    known = [passages, passages_z]
    plane, *sends = pl.pallas_call(
        functools.partial(pick_rows, top, rest),
        out_shape=outs,
        in_specs=[SCALARS] + [WHOLE] * (3 + rest),
        out_specs=[WHOLE] * (1 + top),
        compiler_params=budget(index_rows, index_rows, *outs, *outs),
        cost_estimate=pl.CostEstimate(
            flops=4 * chips * slots * index_rows.shape[0] * width,
            bytes_accessed=3 * index_rows.size * 2, transcendentals=0,
        ),
    )(meta, other_rows, own_rows, passages_z, *asked)

    def send(m, value):
        return exchange(value, ("loop",), 2 * m)

    def over(value):
        return exchange(value, ("rep",), 1)

    def cut(arrays, *pieces):
        return [
            (next(i for i, a in enumerate(arrays) if a is array), first, rows)
            for array, first, rows in pieces
        ]

    half_top = top // 2
    inner, outer = range(1, half_top + 1), range(half_top + 1, top)
    opposite_plane = over(plane)
    middle_masks, late_masks = range(top + 1, chips, 2), range(top, chips, 2)
    sends = dict(zip(range(top, chips), sends))
    middle = [send(m, sends[m]) for m in middle_masks]
    held_back = [sends[m] for m in late_masks]
    known += [exchange(value, ("loop",), 4) for value in known]

    arrays = [plane, opposite_plane, *middle, *known, *held_back]
    quad = [(value, 0, value.shape[0]) for value in known]
    batch, *going = pack(
        [cut(arrays, *[(value, 0, depth) for value in middle])]
        + [
            cut(arrays, (plane, m * depth, depth), (opposite_plane, m * depth, depth),
                *(quad if m == 1 else []))
            for m in inner
        ]
        + [cut(arrays, (value, 0, depth)) for value in held_back],
        *arrays,
    )
    near_batch, far_batch = batch, over(batch)
    came = [send(m, value) for m, value in zip(inner, going)]
    late = [send(m, value) for m, value in zip(late_masks, going[len(inner):])]

    arrays = [plane, opposite_plane, going[0], *late, *came]
    batch, *pair_and_going = pack(
        [cut(arrays, *[(value, 0, depth) for value in late]),
         cut(arrays, (going[0], 2 * depth, 2 * have)),
         cut(arrays, (came[0], 2 * depth, 2 * have))]
        + [
            cut(arrays, (plane, m * depth, depth), (opposite_plane, m * depth, depth))
            for m in outer
        ],
        *arrays, far_batch,
    )
    pair, going = pair_and_going[:2], pair_and_going[2:]
    last = [send(m, value) for m, value in zip(outer, going)] + [over(batch)]
    other_pair = [exchange(value, ("loop",), 1) for value in pair]

    first_rows = [(value, 2 * have) for value in pair]
    first_rows += [(plane, depth), (opposite_plane, depth)]
    first_rows += [(value, 2 * depth) for value in came]
    first_rows += [(value, value.shape[0]) for value in (near_batch, far_batch, batch)]
    last_rows = [(value, value.shape[0]) for value in (*other_pair, *last)]
    first_places = [(m, p) for m in (0, *inner) for p in range(2)]
    first_places += [(m, p) for p in range(2) for m in middle_masks]
    first_places += [(m, 0) for m in late_masks]
    last_places = [(m, p) for m in outer for p in range(2)] + [(m, 1) for m in late_masks]
    side = loop * block // 2
    columns = (
        (tuple(orders[:loop // 2]), tuple(first_places)),
        (tuple(orders[loop // 2:]), tuple(last_places)),
    )
    first_counts = tuple(n for _, n in first_rows)
    last_counts = tuple(n for _, n in last_rows)

    rows = loop * block
    rows_1 = jax.ShapeDtypeStruct((sum(first_counts), width), jnp.bfloat16)
    rows_2 = jax.ShapeDtypeStruct((sum(last_counts), width), jnp.bfloat16)
    payload = jax.ShapeDtypeStruct((side, width + 2 * LOSS), jnp.float32)
    scores, rows_1 = pl.pallas_call(
        functools.partial(early_kernel, first_counts),
        out_shape=[jax.ShapeDtypeStruct((count, rows_1.shape[0]), jnp.float32), rows_1],
        in_specs=[WHOLE] * (1 + len(first_rows)),
        out_specs=[WHOLE] * 2,
        compiler_params=budget(queries, rows_1, rows_1),
        cost_estimate=pl.CostEstimate(
            flops=2 * count * rows_1.size,
            bytes_accessed=2 * (queries.size + 2 * rows_1.size), transcendentals=0,
        ),
    )(queries, *[value for value, _ in first_rows])
    weights_1, weights_2, rows_2, send_part = pl.pallas_call(
        functools.partial(score_kernel, last_counts, len(other_pair), columns, slots),
        out_shape=[
            jax.ShapeDtypeStruct((count, rows_1.shape[0]), jnp.bfloat16),
            jax.ShapeDtypeStruct((count, rows_2.shape[0]), jnp.bfloat16),
            rows_2, payload,
        ],
        in_specs=[SCALARS] * 2 + [WHOLE] * (3 + len(last_rows)),
        out_specs=[WHOLE] * 4,
        compiler_params=budget(queries, rows_2, rows_2, payload, payload),
        cost_estimate=pl.CostEstimate(
            flops=2 * count * (rows_2.size + payload.size),
            bytes_accessed=2 * (queries.size + 2 * rows_2.size) + 4 * payload.size,
            transcendentals=2 * count * (rows_1.shape[0] + rows_2.shape[0]),
        ),
    )(
        meta, hard_counts, queries, positive.reshape(1, count), scores,
        *last, *other_pair,
    )

    sent = exchange(send_part, ("loop",), 1)
    kept = pl.pallas_call(
        keep_kernel,
        out_shape=jax.ShapeDtypeStruct((rows // 2, width + 2 * LOSS), jnp.float32),
        in_specs=[SCALARS] + [WHOLE] * 3,
        out_specs=WHOLE,
        compiler_params=budget(queries, payload, payload),
        cost_estimate=pl.CostEstimate(
            flops=count * rows * width,
            bytes_accessed=2 * count * width + 2 * rows * width, transcendentals=0,
        ),
    )(meta, weights_1, queries, send_part)
    query_grad, done = pl.pallas_call(
        grad_kernel,
        out_shape=[
            jax.ShapeDtypeStruct((count, width), jnp.float32),
            jax.ShapeDtypeStruct((8, 128), jnp.float32),
        ],
        in_specs=[WHOLE] * 4,
        out_specs=[WHOLE] * 2,
        compiler_params=budget(queries, queries, rows_1, rows_2),
        cost_estimate=pl.CostEstimate(
            flops=2 * count * (rows_1.size + rows_2.size),
            bytes_accessed=2 * (rows_1.size + rows_2.size) + 4 * count * width,
            transcendentals=0,
        ),
    )(weights_1, weights_2, rows_1, rows_2)
    part = half + LOSS
    quarter = rows // 4
    first = jax.ShapeDtypeStruct((quarter, part), jnp.float32)
    short = jax.ShapeDtypeStruct(first.shape, jnp.bfloat16)
    own, *going = pl.pallas_call(
        first_sum,
        out_shape=[first, short, first, short],
        in_specs=[WHOLE] * 2,
        out_specs=[WHOLE] * 4,
        compiler_params=budget(payload, payload, payload),
        cost_estimate=pl.CostEstimate(
            flops=payload.size, bytes_accessed=12 * payload.size, transcendentals=0
        ),
    )(kept, sent)
    came = [exchange(value, both, mask) for value, mask in zip(going, (4, 1, 5))]
    second = jax.ShapeDtypeStruct((block, part), jnp.float32)
    total, *going = pl.pallas_call(
        second_sum,
        out_shape=[second] * rest,
        in_specs=[WHOLE] * 5,
        out_specs=[WHOLE] * rest,
        compiler_params=budget(payload, payload),
        cost_estimate=pl.CostEstimate(
            flops=4 * first.size, bytes_accessed=20 * first.size, transcendentals=0
        ),
    )(own, *came, done)
    for value, order in zip(going, orders[1:rest]):
        total = total + exchange(value, ("loop",), order)
    mean_loss = (total[0, half] + total[0, half + LOSS // 2]) / (count * loop * reps)
    total = total[:, :half]
    opposite = exchange(total, ("rep",), 1)
    passage_grad = jnp.where(
        rep == 0,
        jnp.concatenate([total, opposite], axis=1),
        jnp.concatenate([opposite, total], axis=1),
    )

    return (query_grad, passage_grad, mean_loss)


def solution(mesh):
    placed = (
        P(("loop", "rep"), None),
        P("loop", None),
        P(("loop", "rep"), None),
        P(("loop", "rep")),
        P("loop", None, None),
        P("loop", None),
    )
    return jax.shard_map(
        shards,
        mesh=mesh,
        in_specs=placed,
        out_specs=(P(("loop", "rep"), None), P("loop", None), P()),
        check_vma=False,
    )
```

profile of v0, /device:TPU:0, one launch (start us, length us, event | category | flops | bytes accessed | tf_op | source)
XLA Modules:
  0.0 87.7 jit_solution(10702399606922575547)
XLA Ops:
  1.1 2.6 %collective-permute-start.2 = (s32[8,32]{1,0:T(8,128)}, s32[8,32]{1,0:T(8,128)S(1)}, u32[]{:S(2)}, u32[]{:S(2)}) collective-permute-start(s32[8,32]{1,0:T(8,128)} %bitcast.7), channel_id=1, source_target_pairs={{0,4},{2,6},{4,0},{6,2},{8,12},{10,14},{12,8},{14,10},{16,20},{18,... | collective-permute-start | bytes 3080 | tf_op jit(solution)/shard_map/ppermute | solution.py:25
  3.7 2.6 %collective-permute-start.1 = (bf16[8,4096]{1,0:T(8,128)(2,1)}, bf16[8,4096]{1,0:T(8,128)(2,1)S(1)}, u32[]{:S(2)}, u32[]{:S(2)}) collective-permute-start(bf16[8,4096]{1,0:T(8,128)(2,1)} %refs_4_.1), channel_id=1, source_target_pairs={{0,16},{2,18},{4,20},{6,22},{8,24},{10,26},{12,28},{14,30},{16,0},... | collective-permute-start | bytes 196616 | tf_op jit(solution)/shard_map/ppermute | solution.py:25
  8.6 2.3 %collective-permute-start.4 = (s32[16,32]{1,0:T(8,128)S(1)}, s32[16,32]{1,0:T(8,128)S(1)}, u32[]{:S(2)}, u32[]{:S(2)}) collective-permute-start(s32[16,32]{1,0:T(8,128)S(1)} %shard_map.86.refs_0_), channel_id=1, source_target_pairs={{0,16},{2,18},{4,20},{6,22},{8,24},{10,26},{12,28},{14,30},{16,0},... | collective-permute-start | bytes 6152 | tf_op jit(solution)/shard_map/ppermute | solution.py:25
  11.5 1.6 %copy-done.1 = bf16[256,4096]{1,0:T(8,128)(2,1)S(1)} copy-done((bf16[256,4096]{1,0:T(8,128)(2,1)S(1)}, bf16[256,4096]{1,0:T(8,128)(2,1)}, u32[]{:S(2)}) %copy-start.1) | copy-done | bytes 2097176
  13.2 3.1 %collective-permute-done.5.refs_3_ = s32[16,32]{1,0:T(8,128)S(1)} collective-permute-done((s32[16,32]{1,0:T(8,128)S(1)}, s32[16,32]{1,0:T(8,128)S(1)}, u32[]{:S(2)}, u32[]{:S(2)}) %collective-permute-start.5) | collective-permute-done | bytes 2080 | tf_op jit(solution)/shard_map/ppermute | solution.py:25
  17.8 1.6 %collective-permute-start.6 = (bf16[64,4096]{1,0:T(8,128)(2,1)S(1)}, bf16[64,4096]{1,0:T(8,128)(2,1)S(1)}, u32[]{:S(2)}, u32[]{:S(2)}) collective-permute-start(bf16[64,4096]{1,0:T(8,128)(2,1)S(1)} %get-tuple-element.33.refs_0_.refs_2_), channel_id=1, source_target_pairs={{0,1},{1,0},{2,3},{3,2},{4,5},{5,4},{6,7},{7,6},{8,9},{9,8},{10,11... | collective-permute-start | bytes 1572872 | tf_op jit(solution)/shard_map/ppermute | solution.py:25
  19.4 1.9 %collective-permute-start.8 = (bf16[16,4096]{1,0:T(8,128)(2,1)S(1)}, bf16[16,4096]{1,0:T(8,128)(2,1)S(1)}, u32[]{:S(2)}, u32[]{:S(2)}) collective-permute-start(bf16[16,4096]{1,0:T(8,128)(2,1)S(1)} %get-tuple-element.35), channel_id=1, source_target_pairs={{0,28},{2,30},{4,24},{6,26},{8,20},{10,22},{12,16},{14,18},{16,12}... | collective-permute-start | bytes 393224 | tf_op jit(solution)/shard_map/ppermute | solution.py:25
  21.3 2.5 %collective-permute-start.9 = (bf16[8,4096]{1,0:T(8,128)(2,1)S(1)}, bf16[8,4096]{1,0:T(8,128)(2,1)S(1)}, u32[]{:S(2)}, u32[]{:S(2)}) collective-permute-start(bf16[8,4096]{1,0:T(8,128)(2,1)S(1)} %copy-done.2), channel_id=1, source_target_pairs={{0,8},{2,10},{4,12},{6,14},{8,0},{10,2},{12,4},{14,6},{16,24},{18,... | collective-permute-start | bytes 196616 | tf_op jit(solution)/shard_map/ppermute | solution.py:25
  23.8 4.3 %collective-permute-done.9.refs_6_ = bf16[8,4096]{1,0:T(8,128)(2,1)S(1)} collective-permute-done((bf16[8,4096]{1,0:T(8,128)(2,1)S(1)}, bf16[8,4096]{1,0:T(8,128)(2,1)S(1)}, u32[]{:S(2)}, u32[]{:S(2)}) %collective-permute-start.9) | collective-permute-done | bytes 65568 | tf_op jit(solution)/shard_map/ppermute | solution.py:25
  31.2 2.0 %collective-permute-start.14 = (bf16[32,4096]{1,0:T(8,128)(2,1)S(1)}, bf16[32,4096]{1,0:T(8,128)(2,1)S(1)}, u32[]{:S(2)}, u32[]{:S(2)}) collective-permute-start(bf16[32,4096]{1,0:T(8,128)(2,1)S(1)} %get-tuple-element.41), channel_id=1, source_target_pairs={{0,8},{2,10},{4,12},{6,14},{8,0},{10,2},{12,4},{14,6},{16,24},{18,... | collective-permute-start | bytes 786440 | tf_op jit(solution)/shard_map/ppermute | solution.py:25
  34.1 2.7 %collective-permute-start.12 = (bf16[16,4096]{1,0:T(8,128)(2,1)S(1)}, bf16[16,4096]{1,0:T(8,128)(2,1)S(1)}, u32[]{:S(2)}, u32[]{:S(2)}) collective-permute-start(bf16[16,4096]{1,0:T(8,128)(2,1)S(1)} %get-tuple-element.40), channel_id=1, source_target_pairs={{0,24},{2,26},{4,28},{6,30},{8,16},{10,18},{12,20},{14,22},{16,8},... | collective-permute-start | bytes 393224 | tf_op jit(solution)/shard_map/ppermute | solution.py:25
  36.8 4.7 %collective-permute-done.11.refs_3_ = bf16[16,4096]{1,0:T(8,128)(2,1)S(1)} collective-permute-done((bf16[16,4096]{1,0:T(8,128)(2,1)S(1)}, bf16[16,4096]{1,0:T(8,128)(2,1)S(1)}, u32[]{:S(2)}, u32[]{:S(2)}) %collective-permute-start.11) | collective-permute-done | bytes 131104 | tf_op jit(solution)/shard_map/ppermute | solution.py:25
  41.6 4.5 %collective-permute-done.12.refs_4_ = bf16[16,4096]{1,0:T(8,128)(2,1)S(1)} collective-permute-done((bf16[16,4096]{1,0:T(8,128)(2,1)S(1)}, bf16[16,4096]{1,0:T(8,128)(2,1)S(1)}, u32[]{:S(2)}, u32[]{:S(2)}) %collective-permute-start.12) | collective-permute-done | bytes 131104 | tf_op jit(solution)/shard_map/ppermute | solution.py:25
  46.2 1.9 %collective-permute-start.16 = (bf16[32,4096]{1,0:T(8,128)(2,1)S(1)}, bf16[32,4096]{1,0:T(8,128)(2,1)S(1)}, u32[]{:S(2)}, u32[]{:S(2)}) collective-permute-start(bf16[32,4096]{1,0:T(8,128)(2,1)S(1)} %get-tuple-element.47), channel_id=1, source_target_pairs={{0,12},{2,14},{4,8},{6,10},{8,4},{10,6},{12,0},{14,2},{16,28},{18,... | collective-permute-start | bytes 786440 | tf_op jit(solution)/shard_map/ppermute | solution.py:25
  51.0 2.6 %collective-permute-done.16.refs_0_ = bf16[32,4096]{1,0:T(8,128)(2,1)S(1)} collective-permute-done((bf16[32,4096]{1,0:T(8,128)(2,1)S(1)}, bf16[32,4096]{1,0:T(8,128)(2,1)S(1)}, u32[]{:S(2)}, u32[]{:S(2)}) %collective-permute-start.16) | collective-permute-done | bytes 262176 | tf_op jit(solution)/shard_map/ppermute | solution.py:25
  54.5 2.5 %shard_map.91 = (bf16[256,256]{1,0:T(8,128)(2,1)S(1)}, bf16[256,128]{1,0:T(8,128)(2,1)S(1)}, bf16[128,4096]{1,0:T(8,128)(2,1)S(1)}, f32[64,4352]{1,0:T(8,128)S(1)}) custom-call(s32[2]{0:T(128)S(1)} %pad_add_fusion.meta, s32[1,32]{1,0:T(1,128)S(1)} %copy-done.5, bf16[256,4096]{1,0:T(8,128)(2,1)S(1)} %copy-done, s32[1,256]{1,0:T(1,128)S(1)} %bitcast.9, ...), custom_call_target="tpu_custom_call" | custom-call | flops 411041792 | bytes 5308416 | tf_op jit(solution)/shard_map/pallas_call | solution.py:332
  58.1 1.7 %collective-permute-done.20.sent = f32[64,4352]{1,0:T(8,128)S(1)} collective-permute-done((f32[64,4352]{1,0:T(8,128)S(1)}, f32[64,4352]{1,0:T(8,128)S(1)}, u32[]{:S(2)}, u32[]{:S(2)}) %collective-permute-start.20) | collective-permute-done | bytes 1114144 | tf_op jit(solution)/shard_map/ppermute | solution.py:25
  63.5 3.3 %shard_map.92 = (f32[256,4096]{1,0:T(8,128)}, f32[8,128]{1,0:T(8,128)S(1)}) custom-call(bf16[256,256]{1,0:T(8,128)(2,1)S(1)} %get-tuple-element.48.weights_1.weights, bf16[256,128]{1,0:T(8,128)(2,1)S(1)} %get-tuple-element.49.weights_2, bf16[256,4096]{1,0:T(8,128)(2,1)S(1)} %get-tuple-element.50.rows_1, bf16[128,4096]{1,0:T(8,128)(2,1)S(1)} %get-tuple-element.51.rows_2), custom_call_target="tpu_custom_call" | custom-call | flops 805306368 | bytes 7340032 | tf_op jit(solution)/shard_map/pallas_call | solution.py:364
  68.1 1.9 %collective-permute-done.23.from_xy = bf16[32,2176]{1,0:T(8,128)(2,1)S(1)} collective-permute-done((bf16[32,2176]{1,0:T(8,128)(2,1)S(1)}, bf16[32,2176]{1,0:T(8,128)(2,1)S(1)}, u32[]{:S(2)}, u32[]{:S(2)}) %collective-permute-start.23) | collective-permute-done | bytes 139296 | tf_op jit(solution)/shard_map/ppermute | solution.py:25
  70.0 1.7 %collective-permute-done.22.from_y = f32[32,2176]{1,0:T(8,128)S(1)} collective-permute-done((f32[32,2176]{1,0:T(8,128)S(1)}, f32[32,2176]{1,0:T(8,128)S(1)}, u32[]{:S(2)}, u32[]{:S(2)}) %collective-permute-start.22) | collective-permute-done | bytes 278560 | tf_op jit(solution)/shard_map/ppermute | solution.py:25
  73.1 2.4 %collective-permute-start.25 = (f32[8,2176]{1,0:T(8,128)S(1)}, f32[8,2176]{1,0:T(8,128)S(1)}, u32[]{:S(2)}, u32[]{:S(2)}) collective-permute-start(f32[8,2176]{1,0:T(8,128)S(1)} %get-tuple-element.61), channel_id=1, source_target_pairs={{0,8},{2,10},{4,12},{6,14},{8,0},{10,2},{12,4},{14,6},{16,24},{18,... | collective-permute-start | bytes 208904 | tf_op jit(solution)/shard_map/ppermute | solution.py:25
  76.2 2.1 %collective-permute-done.24 = f32[8,2176]{1,0:T(8,128)S(1)} collective-permute-done((f32[8,2176]{1,0:T(8,128)S(1)}, f32[8,2176]{1,0:T(8,128)S(1)}, u32[]{:S(2)}, u32[]{:S(2)}) %collective-permute-start.24) | collective-permute-done | bytes 69664 | tf_op jit(solution)/shard_map/ppermute | solution.py:25
  78.3 3.3 %collective-permute-done.26 = f32[8,2176]{1,0:T(8,128)S(1)} collective-permute-done((f32[8,2176]{1,0:T(8,128)S(1)}, f32[8,2176]{1,0:T(8,128)S(1)}, u32[]{:S(2)}, u32[]{:S(2)}) %collective-permute-start.26) | collective-permute-done | bytes 69664 | tf_op jit(solution)/shard_map/ppermute | solution.py:25
  81.6 1.6 %collective-permute-start.27 = (f32[8,2048]{1,0:T(8,128)S(1)}, f32[8,2048]{1,0:T(8,128)S(1)}, u32[]{:S(2)}, u32[]{:S(2)}) collective-permute-start(f32[8,2048]{1,0:T(8,128)S(1)} %slice.12), channel_id=1, source_target_pairs={{0,1},{1,0},{2,3},{3,2},{4,5},{5,4},{6,7},{7,6},{8,9},{9,8},{10,11... | collective-permute-start | bytes 196616 | tf_op jit(solution)/shard_map/ppermute | solution.py:25
  (60 shorter events, 23.2 us)
Async XLA Ops:
  0.6 15.7 %collective-permute-start = (bf16[256,4096]{1,0:T(8,128)(2,1)}, bf16[256,4096]{1,0:T(8,128)(2,1)S(1)}, u32[]{:S(2)}, u32[]{:S(2)}) collective-permute-start(bf16[256,4096]{1,0:T(8,128)(2,1)} %refs_0_.1), channel_id=1, source_target_pairs={{0,2},{2,0},{4,6},{6,4},{8,10},{10,8},{12,14},{14,12},{16,18},{18,... | collective-permute-start | bytes 6291464 | tf_op jit(solution)/shard_map/ppermute | solution.py:25
  1.1 5.2 %collective-permute-start.2 = (s32[8,32]{1,0:T(8,128)}, s32[8,32]{1,0:T(8,128)S(1)}, u32[]{:S(2)}, u32[]{:S(2)}) collective-permute-start(s32[8,32]{1,0:T(8,128)} %bitcast.7), channel_id=1, source_target_pairs={{0,4},{2,6},{4,0},{6,2},{8,12},{10,14},{12,8},{14,10},{16,20},{18,... | collective-permute-start | bytes 3080 | tf_op jit(solution)/shard_map/ppermute | solution.py:25
  3.7 12.6 %collective-permute-start.1 = (bf16[8,4096]{1,0:T(8,128)(2,1)}, bf16[8,4096]{1,0:T(8,128)(2,1)S(1)}, u32[]{:S(2)}, u32[]{:S(2)}) collective-permute-start(bf16[8,4096]{1,0:T(8,128)(2,1)} %refs_4_.1), channel_id=1, source_target_pairs={{0,16},{2,18},{4,20},{6,22},{8,24},{10,26},{12,28},{14,30},{16,0},... | collective-permute-start | bytes 196616 | tf_op jit(solution)/shard_map/ppermute | solution.py:25
  7.0 6.2 %collective-permute-start.3 = (s32[16,32]{1,0:T(8,128)S(1)}, s32[16,32]{1,0:T(8,128)S(1)}, u32[]{:S(2)}, u32[]{:S(2)}) collective-permute-start(s32[16,32]{1,0:T(8,128)S(1)} %shard_map.86.refs_0_), channel_id=1, source_target_pairs={{0,8},{2,10},{4,12},{6,14},{8,0},{10,2},{12,4},{14,6},{16,24},{18,... | collective-permute-start | bytes 6152 | tf_op jit(solution)/shard_map/ppermute | solution.py:25
  10.9 5.4 %collective-permute-start.5 = (s32[16,32]{1,0:T(8,128)S(1)}, s32[16,32]{1,0:T(8,128)S(1)}, u32[]{:S(2)}, u32[]{:S(2)}) collective-permute-start(s32[16,32]{1,0:T(8,128)S(1)} %shard_map.86.refs_0_), channel_id=1, source_target_pairs={{0,24},{2,26},{4,28},{6,30},{8,16},{10,18},{12,20},{14,22},{16,8},... | collective-permute-start | bytes 6152 | tf_op jit(solution)/shard_map/ppermute | solution.py:25
  17.8 11.7 %collective-permute-start.6 = (bf16[64,4096]{1,0:T(8,128)(2,1)S(1)}, bf16[64,4096]{1,0:T(8,128)(2,1)S(1)}, u32[]{:S(2)}, u32[]{:S(2)}) collective-permute-start(bf16[64,4096]{1,0:T(8,128)(2,1)S(1)} %get-tuple-element.33.refs_0_.refs_2_), channel_id=1, source_target_pairs={{0,1},{1,0},{2,3},{3,2},{4,5},{5,4},{6,7},{7,6},{8,9},{9,8},{10,11... | collective-permute-start | bytes 1572872 | tf_op jit(solution)/shard_map/ppermute | solution.py:25
  19.4 10.2 %collective-permute-start.7 = (bf16[16,4096]{1,0:T(8,128)(2,1)S(1)}, bf16[16,4096]{1,0:T(8,128)(2,1)S(1)}, u32[]{:S(2)}, u32[]{:S(2)}) collective-permute-start(bf16[16,4096]{1,0:T(8,128)(2,1)S(1)} %get-tuple-element.34), channel_id=1, source_target_pairs={{0,20},{2,22},{4,16},{6,18},{8,28},{10,30},{12,24},{14,26},{16,4},... | collective-permute-start | bytes 393224 | tf_op jit(solution)/shard_map/ppermute | solution.py:25
  19.4 10.1 %collective-permute-start.8 = (bf16[16,4096]{1,0:T(8,128)(2,1)S(1)}, bf16[16,4096]{1,0:T(8,128)(2,1)S(1)}, u32[]{:S(2)}, u32[]{:S(2)}) collective-permute-start(bf16[16,4096]{1,0:T(8,128)(2,1)S(1)} %get-tuple-element.35), channel_id=1, source_target_pairs={{0,28},{2,30},{4,24},{6,26},{8,20},{10,22},{12,16},{14,18},{16,12}... | collective-permute-start | bytes 393224 | tf_op jit(solution)/shard_map/ppermute | solution.py:25
  21.3 6.8 %collective-permute-start.9 = (bf16[8,4096]{1,0:T(8,128)(2,1)S(1)}, bf16[8,4096]{1,0:T(8,128)(2,1)S(1)}, u32[]{:S(2)}, u32[]{:S(2)}) collective-permute-start(bf16[8,4096]{1,0:T(8,128)(2,1)S(1)} %copy-done.2), channel_id=1, source_target_pairs={{0,8},{2,10},{4,12},{6,14},{8,0},{10,2},{12,4},{14,6},{16,24},{18,... | collective-permute-start | bytes 196616 | tf_op jit(solution)/shard_map/ppermute | solution.py:25
  23.8 5.8 %collective-permute-start.10 = (bf16[8,4096]{1,0:T(8,128)(2,1)S(1)}, bf16[8,4096]{1,0:T(8,128)(2,1)S(1)}, u32[]{:S(2)}, u32[]{:S(2)}) collective-permute-start(bf16[8,4096]{1,0:T(8,128)(2,1)S(1)} %collective-permute-done.1.after.refs_5_), channel_id=1, source_target_pairs={{0,8},{2,10},{4,12},{6,14},{8,0},{10,2},{12,4},{14,6},{16,24},{18,... | collective-permute-start | bytes 196616 | tf_op jit(solution)/shard_map/ppermute | solution.py:25
  29.7 16.5 %collective-permute-start.13 = (bf16[64,4096]{1,0:T(8,128)(2,1)S(1)}, bf16[64,4096]{1,0:T(8,128)(2,1)S(1)}, u32[]{:S(2)}, u32[]{:S(2)}) collective-permute-start(bf16[64,4096]{1,0:T(8,128)(2,1)S(1)} %get-tuple-element.38.refs_2_), channel_id=1, source_target_pairs={{0,4},{2,6},{4,0},{6,2},{8,12},{10,14},{12,8},{14,10},{16,20},{18,... | collective-permute-start | bytes 1572872 | tf_op jit(solution)/shard_map/ppermute | solution.py:25
  31.2 15.0 %collective-permute-start.14 = (bf16[32,4096]{1,0:T(8,128)(2,1)S(1)}, bf16[32,4096]{1,0:T(8,128)(2,1)S(1)}, u32[]{:S(2)}, u32[]{:S(2)}) collective-permute-start(bf16[32,4096]{1,0:T(8,128)(2,1)S(1)} %get-tuple-element.41), channel_id=1, source_target_pairs={{0,8},{2,10},{4,12},{6,14},{8,0},{10,2},{12,4},{14,6},{16,24},{18,... | collective-permute-start | bytes 786440 | tf_op jit(solution)/shard_map/ppermute | solution.py:25
  33.1 13.0 %collective-permute-start.15 = (bf16[32,4096]{1,0:T(8,128)(2,1)S(1)}, bf16[32,4096]{1,0:T(8,128)(2,1)S(1)}, u32[]{:S(2)}, u32[]{:S(2)}) collective-permute-start(bf16[32,4096]{1,0:T(8,128)(2,1)S(1)} %get-tuple-element.42.refs_6_), channel_id=1, source_target_pairs={{0,1},{1,0},{2,3},{3,2},{4,5},{5,4},{6,7},{7,6},{8,9},{9,8},{10,11... | collective-permute-start | bytes 786440 | tf_op jit(solution)/shard_map/ppermute | solution.py:25
  33.7 7.9 %collective-permute-start.11 = (bf16[16,4096]{1,0:T(8,128)(2,1)S(1)}, bf16[16,4096]{1,0:T(8,128)(2,1)S(1)}, u32[]{:S(2)}, u32[]{:S(2)}) collective-permute-start(bf16[16,4096]{1,0:T(8,128)(2,1)S(1)} %get-tuple-element.39), channel_id=1, source_target_pairs={{0,16},{2,18},{4,20},{6,22},{8,24},{10,26},{12,28},{14,30},{16,0},... | collective-permute-start | bytes 393224 | tf_op jit(solution)/shard_map/ppermute | solution.py:25
  34.1 12.0 %collective-permute-start.12 = (bf16[16,4096]{1,0:T(8,128)(2,1)S(1)}, bf16[16,4096]{1,0:T(8,128)(2,1)S(1)}, u32[]{:S(2)}, u32[]{:S(2)}) collective-permute-start(bf16[16,4096]{1,0:T(8,128)(2,1)S(1)} %get-tuple-element.40), channel_id=1, source_target_pairs={{0,24},{2,26},{4,28},{6,30},{8,16},{10,18},{12,20},{14,22},{16,8},... | collective-permute-start | bytes 393224 | tf_op jit(solution)/shard_map/ppermute | solution.py:25
  46.2 7.3 %collective-permute-start.16 = (bf16[32,4096]{1,0:T(8,128)(2,1)S(1)}, bf16[32,4096]{1,0:T(8,128)(2,1)S(1)}, u32[]{:S(2)}, u32[]{:S(2)}) collective-permute-start(bf16[32,4096]{1,0:T(8,128)(2,1)S(1)} %get-tuple-element.47), channel_id=1, source_target_pairs={{0,12},{2,14},{4,8},{6,10},{8,4},{10,6},{12,0},{14,2},{16,28},{18,... | collective-permute-start | bytes 786440 | tf_op jit(solution)/shard_map/ppermute | solution.py:25
  48.1 6.4 %collective-permute-start.17 = (bf16[32,4096]{1,0:T(8,128)(2,1)S(1)}, bf16[32,4096]{1,0:T(8,128)(2,1)S(1)}, u32[]{:S(2)}, u32[]{:S(2)}) collective-permute-start(bf16[32,4096]{1,0:T(8,128)(2,1)S(1)} %get-tuple-element.45.refs_8_), channel_id=1, source_target_pairs={{0,1},{1,0},{2,3},{3,2},{4,5},{5,4},{6,7},{7,6},{8,9},{9,8},{10,11... | collective-permute-start | bytes 786440 | tf_op jit(solution)/shard_map/ppermute | solution.py:25
  49.6 4.9 %collective-permute-start.18 = (bf16[32,4096]{1,0:T(8,128)(2,1)S(1)}, bf16[32,4096]{1,0:T(8,128)(2,1)S(1)}, u32[]{:S(2)}, u32[]{:S(2)}) collective-permute-start(bf16[32,4096]{1,0:T(8,128)(2,1)S(1)} %get-tuple-element.43.refs_0_), channel_id=1, source_target_pairs={{0,2},{2,0},{4,6},{6,4},{8,10},{10,8},{12,14},{14,12},{16,18},{18,... | collective-permute-start | bytes 786440 | tf_op jit(solution)/shard_map/ppermute | solution.py:25
  59.9 11.7 %collective-permute-start.22 = (f32[32,2176]{1,0:T(8,128)S(1)}, f32[32,2176]{1,0:T(8,128)S(1)}, u32[]{:S(2)}, u32[]{:S(2)}) collective-permute-start(f32[32,2176]{1,0:T(8,128)S(1)} %get-tuple-element.56), channel_id=1, source_target_pairs={{0,1},{1,0},{2,3},{3,2},{4,5},{5,4},{6,7},{7,6},{8,9},{9,8},{10,11... | collective-permute-start | bytes 835592 | tf_op jit(solution)/shard_map/ppermute | solution.py:25
  61.5 6.6 %collective-permute-start.21 = (bf16[32,2176]{1,0:T(8,128)(2,1)S(1)}, bf16[32,2176]{1,0:T(8,128)(2,1)S(1)}, u32[]{:S(2)}, u32[]{:S(2)}) collective-permute-start(bf16[32,2176]{1,0:T(8,128)(2,1)S(1)} %get-tuple-element.55), channel_id=1, source_target_pairs={{0,4},{1,5},{2,6},{3,7},{4,0},{5,1},{6,2},{7,3},{8,12},{9,13},{10,... | collective-permute-start | bytes 417800 | tf_op jit(solution)/shard_map/ppermute | solution.py:25
  61.9 8.1 %collective-permute-start.23 = (bf16[32,2176]{1,0:T(8,128)(2,1)S(1)}, bf16[32,2176]{1,0:T(8,128)(2,1)S(1)}, u32[]{:S(2)}, u32[]{:S(2)}) collective-permute-start(bf16[32,2176]{1,0:T(8,128)(2,1)S(1)} %get-tuple-element.57), channel_id=1, source_target_pairs={{0,5},{1,4},{2,7},{3,6},{4,1},{5,0},{6,3},{7,2},{8,13},{9,12},{10,... | collective-permute-start | bytes 417800 | tf_op jit(solution)/shard_map/ppermute | solution.py:25
  71.7 6.6 %collective-permute-start.24 = (f32[8,2176]{1,0:T(8,128)S(1)}, f32[8,2176]{1,0:T(8,128)S(1)}, u32[]{:S(2)}, u32[]{:S(2)}) collective-permute-start(f32[8,2176]{1,0:T(8,128)S(1)} %get-tuple-element.60), channel_id=1, source_target_pairs={{0,16},{2,18},{4,20},{6,22},{8,24},{10,26},{12,28},{14,30},{16,0},... | collective-permute-start | bytes 208904 | tf_op jit(solution)/shard_map/ppermute | solution.py:25
  73.1 5.2 %collective-permute-start.25 = (f32[8,2176]{1,0:T(8,128)S(1)}, f32[8,2176]{1,0:T(8,128)S(1)}, u32[]{:S(2)}, u32[]{:S(2)}) collective-permute-start(f32[8,2176]{1,0:T(8,128)S(1)} %get-tuple-element.61), channel_id=1, source_target_pairs={{0,8},{2,10},{4,12},{6,14},{8,0},{10,2},{12,4},{14,6},{16,24},{18,... | collective-permute-start | bytes 208904 | tf_op jit(solution)/shard_map/ppermute | solution.py:25
  75.5 6.1 %collective-permute-start.26 = (f32[8,2176]{1,0:T(8,128)S(1)}, f32[8,2176]{1,0:T(8,128)S(1)}, u32[]{:S(2)}, u32[]{:S(2)}) collective-permute-start(f32[8,2176]{1,0:T(8,128)S(1)} %get-tuple-element.62), channel_id=1, source_target_pairs={{0,24},{2,26},{4,28},{6,30},{8,16},{10,18},{12,20},{14,22},{16,8},... | collective-permute-start | bytes 208904 | tf_op jit(solution)/shard_map/ppermute | solution.py:25
  (10 other events, 57.4 us)
where the time goes:
time: 88 us; the launch traced here: 87.7 us
  starting transfers between devices  36.9 us (42%)
  waiting for transfers between devices  34.5 us (39%)
  Pallas kernels  9.49 us (11%)
  between operations  3.21 us (4%)
  local copies, waits for them, and re-layouts  2.89 us (3%)
    ppermute x28, starting transfers between devices, exchange(): return lax.ppermute(value, axes, [(i, i ^ mask) for i in range(size)])  36.9 us
    ppermute x28, waiting for transfers between devices, exchange(): return lax.ppermute(value, axes, [(i, i ^ mask) for i in range(size)])  34.5 us
    pallas_call x1, Pallas kernels, shards(): pl.pallas_call(grad_kernel, out_shape=[jax.ShapeDtypeStruct((count, width...  3.28 us
    pallas_call x1, Pallas kernels, shards(): pl.pallas_call(functools.partial(score_kernel, last_counts, len(other_pai...  2.45 us
    unnamed x12, local copies, waits for them, and re-layouts  2.3 us
  transfers between devices with their start and end apart: 28, of which 14 were waited for; matrix products, arithmetic and copies ran while one was open for 1% of the time, Pallas kernels for 6%

commit v1 on v0

--- a/solution.py
+++ b/solution.py
@@ -183,12 +183,19 @@
 
 
 def second_sum(own, from_x, from_y, from_xy, after, *outs):
-    rows = outs[0].shape[0]
+    rows, columns = outs[0].shape
+    half = columns - LOSS
+    lanes = lax.broadcasted_iota(jnp.int32, (rows, LOSS), 1)
     for i, out in enumerate(outs):
         at = pl.ds(i * rows, rows)
-        out[...] = (own[at] + from_x[at].astype(jnp.float32)) + (
-            from_y[at].astype(jnp.float32) + from_xy[at].astype(jnp.float32)
-        )
+        total = (own[at] + from_x[at]) + (from_y[at] + from_xy[at].astype(jnp.float32))
+        if out.dtype == jnp.float32:
+            out[...] = total
+        else:
+            loss = total[:, half:half + 1] + total[:, half + LOSS // 2:half + LOSS // 2 + 1]
+            high = loss.astype(jnp.bfloat16).astype(jnp.float32)
+            out[:, :half] = total[:, :half].astype(out.dtype)
+            out[:, half:] = jnp.where(lanes < LOSS // 2, high, loss - high).astype(out.dtype)
 
 
 def grad_kernel(weights_1, weights_2, rows_1, rows_2, out, done):
@@ -215,7 +222,8 @@
     other_rows = exchange(index_rows, ("loop",), 1)
     rest = loop // 4
     wanted = jnp.transpose(hard_rows, (0, 2, 1)).reshape(slots, owners)
-    asked, = pack([[(0, 0, slots), (1, 0, slots)]], wanted, exchange(wanted, ("loop",), 2))
+    neighbour, (own_wanted,) = exchange(wanted, ("loop",), 2), pack([[(0, 0, slots)]], wanted)
+    asked, = pack([[(0, 0, slots), (1, 0, slots)]], own_wanted, neighbour)
     asked = [asked] + [exchange(asked, ("loop",), 4 * k) for k in range(1, rest)]
     own_rows, = pack([[(0, 0, index_rows.shape[0])]], index_rows)
 
@@ -232,7 +240,7 @@
     top = chips // 2
     outs = [jax.ShapeDtypeStruct((top * depth, width), jnp.bfloat16)]
     outs += [jax.ShapeDtypeStruct((depth, width), jnp.bfloat16)] * top
-    known = [passages, passages_z]
+    known, = pack([[(i, 0, have // 2) for i in range(2)]], passages, passages_z)
     plane, *sends = pl.pallas_call(
         functools.partial(pick_rows, top, rest),
         out_shape=outs,
@@ -264,7 +272,7 @@
     sends = dict(zip(range(top, chips), sends))
     middle = [send(m, sends[m]) for m in middle_masks]
     held_back = [sends[m] for m in late_masks]
-    known += [exchange(value, ("loop",), 4) for value in known]
+    known = [known, exchange(known, ("loop",), 4)]
 
     arrays = [plane, opposite_plane, *middle, *known, *held_back]
     quad = [(value, 0, value.shape[0]) for value in known]
@@ -382,7 +390,7 @@
     short = jax.ShapeDtypeStruct(first.shape, jnp.bfloat16)
     own, *going = pl.pallas_call(
         first_sum,
-        out_shape=[first, short, first, short],
+        out_shape=[first, first, first, short],
         in_specs=[WHOLE] * 2,
         out_specs=[WHOLE] * 4,
         compiler_params=budget(payload, payload, payload),
@@ -394,7 +402,7 @@
     second = jax.ShapeDtypeStruct((block, part), jnp.float32)
     total, *going = pl.pallas_call(
         second_sum,
-        out_shape=[second] * rest,
+        out_shape=[second] * (rest - 1) + [jax.ShapeDtypeStruct(second.shape, jnp.bfloat16)],
         in_specs=[WHOLE] * 5,
         out_specs=[WHOLE] * rest,
         compiler_params=budget(payload, payload),
@@ -403,7 +411,7 @@
         ),
     )(own, *came, done)
     for value, order in zip(going, orders[1:rest]):
-        total = total + exchange(value, ("loop",), order)
+        total = total + exchange(value, ("loop",), order).astype(jnp.float32)
     mean_loss = (total[0, half] + total[0, half + LOSS // 2]) / (count * loop * reps)
     total = total[:, :half]
     opposite = exchange(total, ("rep",), 1)

time: 88 us -> 86.1 us (0.978)
  waiting for transfers between devices: 34.5 us -> 32.8 us
    ppermute x28 -> x27, waiting for transfers between devices: 34.5 us -> 32.8 us  [exchange(): return lax.ppermute(value, axes, [(i, i ^ mask) for i in range(size)])]
    ppermute x28 -> x27, starting transfers between devices: 36.9 us -> 36.6 us  [exchange(): return lax.ppermute(value, axes, [(i, i ^ mask) for i in range(size)])]
  transfers between devices with their start and end apart: 28 -> 27, of which waited for: 14 -> 11; matrix products, arithmetic and copies ran while one was open for 1% -> 1% of each run, Pallas kernels for 6% -> 6%
where the time goes in v1:
time: 86.1 us; the launch traced here: 85.9 us
  starting transfers between devices  36.6 us (43%)
  waiting for transfers between devices  32.8 us (38%)
  Pallas kernels  9.59 us (11%)
  between operations  3.22 us (4%)
  local copies, waits for them, and re-layouts  2.88 us (3%)
    ppermute x27, starting transfers between devices, exchange(): return lax.ppermute(value, axes, [(i, i ^ mask) for i in range(size)])  36.6 us
    ppermute x27, waiting for transfers between devices, exchange(): return lax.ppermute(value, axes, [(i, i ^ mask) for i in range(size)])  32.8 us
    pallas_call x1, Pallas kernels, shards(): pl.pallas_call(grad_kernel, out_shape=[jax.ShapeDtypeStruct((count, width...  3.28 us
    pallas_call x1, Pallas kernels, shards(): pl.pallas_call(functools.partial(score_kernel, last_counts, len(other_pai...  2.45 us
    unnamed x12, local copies, waits for them, and re-layouts  2.29 us
  transfers between devices with their start and end apart: 27, of which 11 were waited for; matrix products, arithmetic and copies ran while one was open for 1% of the time, Pallas kernels for 6%

profile of v1, /device:TPU:0, one launch (start us, length us, event | category | flops | bytes accessed | tf_op | source)
XLA Modules:
  0.0 85.9 jit_solution(5552927622733759801)
XLA Ops:
  1.1 2.6 %collective-permute-start.2 = (s32[8,32]{1,0:T(8,128)}, s32[8,32]{1,0:T(8,128)S(1)}, u32[]{:S(2)}, u32[]{:S(2)}) collective-permute-start(s32[8,32]{1,0:T(8,128)} %bitcast.7), channel_id=1, source_target_pairs={{0,4},{2,6},{4,0},{6,2},{8,12},{10,14},{12,8},{14,10},{16,20},{18,... | collective-permute-start | bytes 3080 | tf_op jit(solution)/shard_map/ppermute | solution.py:25
  3.7 2.6 %collective-permute-start.1 = (bf16[8,4096]{1,0:T(8,128)(2,1)}, bf16[8,4096]{1,0:T(8,128)(2,1)S(1)}, u32[]{:S(2)}, u32[]{:S(2)}) collective-permute-start(bf16[8,4096]{1,0:T(8,128)(2,1)} %refs_0_.3), channel_id=1, source_target_pairs={{0,16},{2,18},{4,20},{6,22},{8,24},{10,26},{12,28},{14,30},{16,0},... | collective-permute-start | bytes 196616 | tf_op jit(solution)/shard_map/ppermute | solution.py:25
  7.0 1.6 %collective-permute-start.3 = (s32[16,32]{1,0:T(8,128)S(1)}, s32[16,32]{1,0:T(8,128)S(1)}, u32[]{:S(2)}, u32[]{:S(2)}) collective-permute-start(s32[16,32]{1,0:T(8,128)S(1)} %shard_map.87.refs_0_), channel_id=1, source_target_pairs={{0,8},{2,10},{4,12},{6,14},{8,0},{10,2},{12,4},{14,6},{16,24},{18,... | collective-permute-start | bytes 6152 | tf_op jit(solution)/shard_map/ppermute | solution.py:25
  8.6 1.6 %collective-permute-start.4 = (s32[16,32]{1,0:T(8,128)S(1)}, s32[16,32]{1,0:T(8,128)S(1)}, u32[]{:S(2)}, u32[]{:S(2)}) collective-permute-start(s32[16,32]{1,0:T(8,128)S(1)} %shard_map.87.refs_0_), channel_id=1, source_target_pairs={{0,16},{2,18},{4,20},{6,22},{8,24},{10,26},{12,28},{14,30},{16,0},... | collective-permute-start | bytes 6152 | tf_op jit(solution)/shard_map/ppermute | solution.py:25
  11.5 1.6 %copy-done.1 = bf16[256,4096]{1,0:T(8,128)(2,1)S(1)} copy-done((bf16[256,4096]{1,0:T(8,128)(2,1)S(1)}, bf16[256,4096]{1,0:T(8,128)(2,1)}, u32[]{:S(2)}) %copy-start.1) | copy-done | bytes 2097176
  13.3 2.4 %collective-permute-done.5.refs_3_ = s32[16,32]{1,0:T(8,128)S(1)} collective-permute-done((s32[16,32]{1,0:T(8,128)S(1)}, s32[16,32]{1,0:T(8,128)S(1)}, u32[]{:S(2)}, u32[]{:S(2)}) %collective-permute-start.5) | collective-permute-done | bytes 2080 | tf_op jit(solution)/shard_map/ppermute | solution.py:25
  17.1 1.6 %collective-permute-start.6 = (bf16[64,4096]{1,0:T(8,128)(2,1)S(1)}, bf16[64,4096]{1,0:T(8,128)(2,1)S(1)}, u32[]{:S(2)}, u32[]{:S(2)}) collective-permute-start(bf16[64,4096]{1,0:T(8,128)(2,1)S(1)} %get-tuple-element.33.refs_0_.refs_2_), channel_id=1, source_target_pairs={{0,1},{1,0},{2,3},{3,2},{4,5},{5,4},{6,7},{7,6},{8,9},{9,8},{10,11... | collective-permute-start | bytes 1572872 | tf_op jit(solution)/shard_map/ppermute | solution.py:25
  18.8 1.8 %collective-permute-start.7 = (bf16[16,4096]{1,0:T(8,128)(2,1)S(1)}, bf16[16,4096]{1,0:T(8,128)(2,1)S(1)}, u32[]{:S(2)}, u32[]{:S(2)}) collective-permute-start(bf16[16,4096]{1,0:T(8,128)(2,1)S(1)} %get-tuple-element.34), channel_id=1, source_target_pairs={{0,20},{2,22},{4,16},{6,18},{8,28},{10,30},{12,24},{14,26},{16,4},... | collective-permute-start | bytes 393224 | tf_op jit(solution)/shard_map/ppermute | solution.py:25
  20.6 3.5 %collective-permute-start.8 = (bf16[16,4096]{1,0:T(8,128)(2,1)S(1)}, bf16[16,4096]{1,0:T(8,128)(2,1)S(1)}, u32[]{:S(2)}, u32[]{:S(2)}) collective-permute-start(bf16[16,4096]{1,0:T(8,128)(2,1)S(1)} %get-tuple-element.35), channel_id=1, source_target_pairs={{0,28},{2,30},{4,24},{6,26},{8,20},{10,22},{12,16},{14,18},{16,12}... | collective-permute-start | bytes 393224 | tf_op jit(solution)/shard_map/ppermute | solution.py:25
  24.1 6.4 %collective-permute-done.7.refs_2_ = bf16[16,4096]{1,0:T(8,128)(2,1)S(1)} collective-permute-done((bf16[16,4096]{1,0:T(8,128)(2,1)S(1)}, bf16[16,4096]{1,0:T(8,128)(2,1)S(1)}, u32[]{:S(2)}, u32[]{:S(2)}) %collective-permute-start.7) | collective-permute-done | bytes 131104 | tf_op jit(solution)/shard_map/ppermute | solution.py:25
  30.6 1.5 %collective-permute-start.12 = (bf16[64,4096]{1,0:T(8,128)(2,1)S(1)}, bf16[64,4096]{1,0:T(8,128)(2,1)S(1)}, u32[]{:S(2)}, u32[]{:S(2)}) collective-permute-start(bf16[64,4096]{1,0:T(8,128)(2,1)S(1)} %get-tuple-element.38.refs_2_), channel_id=1, source_target_pairs={{0,4},{2,6},{4,0},{6,2},{8,12},{10,14},{12,8},{14,10},{16,20},{18,... | collective-permute-start | bytes 1572872 | tf_op jit(solution)/shard_map/ppermute | solution.py:25
  32.1 1.9 %collective-permute-start.13 = (bf16[32,4096]{1,0:T(8,128)(2,1)S(1)}, bf16[32,4096]{1,0:T(8,128)(2,1)S(1)}, u32[]{:S(2)}, u32[]{:S(2)}) collective-permute-start(bf16[32,4096]{1,0:T(8,128)(2,1)S(1)} %get-tuple-element.41), channel_id=1, source_target_pairs={{0,8},{2,10},{4,12},{6,14},{8,0},{10,2},{12,4},{14,6},{16,24},{18,... | collective-permute-start | bytes 786440 | tf_op jit(solution)/shard_map/ppermute | solution.py:25
  34.5 2.5 %collective-permute-start.11 = (bf16[16,4096]{1,0:T(8,128)(2,1)S(1)}, bf16[16,4096]{1,0:T(8,128)(2,1)S(1)}, u32[]{:S(2)}, u32[]{:S(2)}) collective-permute-start(bf16[16,4096]{1,0:T(8,128)(2,1)S(1)} %get-tuple-element.40), channel_id=1, source_target_pairs={{0,24},{2,26},{4,28},{6,30},{8,16},{10,18},{12,20},{14,22},{16,8},... | collective-permute-start | bytes 393224 | tf_op jit(solution)/shard_map/ppermute | solution.py:25
  37.1 4.7 %collective-permute-done.10.refs_3_ = bf16[16,4096]{1,0:T(8,128)(2,1)S(1)} collective-permute-done((bf16[16,4096]{1,0:T(8,128)(2,1)S(1)}, bf16[16,4096]{1,0:T(8,128)(2,1)S(1)}, u32[]{:S(2)}, u32[]{:S(2)}) %collective-permute-start.10) | collective-permute-done | bytes 131104 | tf_op jit(solution)/shard_map/ppermute | solution.py:25
  41.8 3.3 %collective-permute-done.11.refs_4_ = bf16[16,4096]{1,0:T(8,128)(2,1)S(1)} collective-permute-done((bf16[16,4096]{1,0:T(8,128)(2,1)S(1)}, bf16[16,4096]{1,0:T(8,128)(2,1)S(1)}, u32[]{:S(2)}, u32[]{:S(2)}) %collective-permute-start.11) | collective-permute-done | bytes 131104 | tf_op jit(solution)/shard_map/ppermute | solution.py:25
  49.5 3.0 %collective-permute-done.15.refs_0_ = bf16[32,4096]{1,0:T(8,128)(2,1)S(1)} collective-permute-done((bf16[32,4096]{1,0:T(8,128)(2,1)S(1)}, bf16[32,4096]{1,0:T(8,128)(2,1)S(1)}, u32[]{:S(2)}, u32[]{:S(2)}) %collective-permute-start.15) | collective-permute-done | bytes 262176 | tf_op jit(solution)/shard_map/ppermute | solution.py:25
  53.1 2.5 %shard_map.93 = (bf16[256,256]{1,0:T(8,128)(2,1)S(1)}, bf16[256,128]{1,0:T(8,128)(2,1)S(1)}, bf16[128,4096]{1,0:T(8,128)(2,1)S(1)}, f32[64,4352]{1,0:T(8,128)S(1)}) custom-call(s32[2]{0:T(128)S(1)} %pad_add_fusion.meta, s32[1,32]{1,0:T(1,128)S(1)} %copy-done.5, bf16[256,4096]{1,0:T(8,128)(2,1)S(1)} %copy-done, s32[1,256]{1,0:T(1,128)S(1)} %bitcast.9, ...), custom_call_target="tpu_custom_call" | custom-call | flops 411041792 | bytes 5308416 | tf_op jit(solution)/shard_map/pallas_call | solution.py:340
  56.7 1.7 %collective-permute-done.19.sent = f32[64,4352]{1,0:T(8,128)S(1)} collective-permute-done((f32[64,4352]{1,0:T(8,128)S(1)}, f32[64,4352]{1,0:T(8,128)S(1)}, u32[]{:S(2)}, u32[]{:S(2)}) %collective-permute-start.19) | collective-permute-done | bytes 1114144 | tf_op jit(solution)/shard_map/ppermute | solution.py:25
  58.5 1.5 %collective-permute-start.20 = (f32[32,2176]{1,0:T(8,128)S(1)}, f32[32,2176]{1,0:T(8,128)S(1)}, u32[]{:S(2)}, u32[]{:S(2)}) collective-permute-start(f32[32,2176]{1,0:T(8,128)S(1)} %get-tuple-element.55), channel_id=1, source_target_pairs={{0,4},{1,5},{2,6},{3,7},{4,0},{5,1},{6,2},{7,3},{8,12},{9,13},{10,... | collective-permute-start | bytes 835592 | tf_op jit(solution)/shard_map/ppermute | solution.py:25
  62.0 3.3 %shard_map.94 = (f32[256,4096]{1,0:T(8,128)}, f32[8,128]{1,0:T(8,128)S(1)}) custom-call(bf16[256,256]{1,0:T(8,128)(2,1)S(1)} %get-tuple-element.48.weights_1.weights, bf16[256,128]{1,0:T(8,128)(2,1)S(1)} %get-tuple-element.49.weights_2, bf16[256,4096]{1,0:T(8,128)(2,1)S(1)} %get-tuple-element.50.rows_1, bf16[128,4096]{1,0:T(8,128)(2,1)S(1)} %get-tuple-element.51.rows_2), custom_call_target="tpu_custom_call" | custom-call | flops 805306368 | bytes 7340032 | tf_op jit(solution)/shard_map/pallas_call | solution.py:372
  65.3 6.0 %collective-permute-done.22.from_xy = bf16[32,2176]{1,0:T(8,128)(2,1)S(1)} collective-permute-done((bf16[32,2176]{1,0:T(8,128)(2,1)S(1)}, bf16[32,2176]{1,0:T(8,128)(2,1)S(1)}, u32[]{:S(2)}, u32[]{:S(2)}) %collective-permute-start.22) | collective-permute-done | bytes 139296 | tf_op jit(solution)/shard_map/ppermute | solution.py:25
  74.0 2.0 %collective-permute-start.25 = (bf16[8,2176]{1,0:T(8,128)(2,1)S(1)}, bf16[8,2176]{1,0:T(8,128)(2,1)S(1)}, u32[]{:S(2)}, u32[]{:S(2)}) collective-permute-start(bf16[8,2176]{1,0:T(8,128)(2,1)S(1)} %get-tuple-element.62), channel_id=1, source_target_pairs={{0,24},{2,26},{4,28},{6,30},{8,16},{10,18},{12,20},{14,22},{16,8},... | collective-permute-start | bytes 104456 | tf_op jit(solution)/shard_map/ppermute | solution.py:25
  76.0 3.7 %collective-permute-done.25 = bf16[8,2176]{1,0:T(8,128)(2,1)S(1)} collective-permute-done((bf16[8,2176]{1,0:T(8,128)(2,1)S(1)}, bf16[8,2176]{1,0:T(8,128)(2,1)S(1)}, u32[]{:S(2)}, u32[]{:S(2)}) %collective-permute-start.25) | collective-permute-done | bytes 34848 | tf_op jit(solution)/shard_map/ppermute | solution.py:25
  79.7 1.5 %collective-permute-start.26 = (f32[8,2048]{1,0:T(8,128)S(1)}, f32[8,2048]{1,0:T(8,128)S(1)}, u32[]{:S(2)}, u32[]{:S(2)}) collective-permute-start(f32[8,2048]{1,0:T(8,128)S(1)} %slice.12), channel_id=1, source_target_pairs={{0,1},{1,0},{2,3},{3,2},{4,5},{5,4},{6,7},{7,6},{8,9},{9,8},{10,11... | collective-permute-start | bytes 196616 | tf_op jit(solution)/shard_map/ppermute | solution.py:25
  (60 shorter events, 17.9 us)
Async XLA Ops:
  0.6 15.0 %collective-permute-start = (bf16[256,4096]{1,0:T(8,128)(2,1)}, bf16[256,4096]{1,0:T(8,128)(2,1)S(1)}, u32[]{:S(2)}, u32[]{:S(2)}) collective-permute-start(bf16[256,4096]{1,0:T(8,128)(2,1)} %refs_0_.2), channel_id=1, source_target_pairs={{0,2},{2,0},{4,6},{6,4},{8,10},{10,8},{12,14},{14,12},{16,18},{18,... | collective-permute-start | bytes 6291464 | tf_op jit(solution)/shard_map/ppermute | solution.py:25
  1.1 5.8 %collective-permute-start.2 = (s32[8,32]{1,0:T(8,128)}, s32[8,32]{1,0:T(8,128)S(1)}, u32[]{:S(2)}, u32[]{:S(2)}) collective-permute-start(s32[8,32]{1,0:T(8,128)} %bitcast.7), channel_id=1, source_target_pairs={{0,4},{2,6},{4,0},{6,2},{8,12},{10,14},{12,8},{14,10},{16,20},{18,... | collective-permute-start | bytes 3080 | tf_op jit(solution)/shard_map/ppermute | solution.py:25
  3.7 11.9 %collective-permute-start.1 = (bf16[8,4096]{1,0:T(8,128)(2,1)}, bf16[8,4096]{1,0:T(8,128)(2,1)S(1)}, u32[]{:S(2)}, u32[]{:S(2)}) collective-permute-start(bf16[8,4096]{1,0:T(8,128)(2,1)} %refs_0_.3), channel_id=1, source_target_pairs={{0,16},{2,18},{4,20},{6,22},{8,24},{10,26},{12,28},{14,30},{16,0},... | collective-permute-start | bytes 196616 | tf_op jit(solution)/shard_map/ppermute | solution.py:25
  7.0 6.3 %collective-permute-start.3 = (s32[16,32]{1,0:T(8,128)S(1)}, s32[16,32]{1,0:T(8,128)S(1)}, u32[]{:S(2)}, u32[]{:S(2)}) collective-permute-start(s32[16,32]{1,0:T(8,128)S(1)} %shard_map.87.refs_0_), channel_id=1, source_target_pairs={{0,8},{2,10},{4,12},{6,14},{8,0},{10,2},{12,4},{14,6},{16,24},{18,... | collective-permute-start | bytes 6152 | tf_op jit(solution)/shard_map/ppermute | solution.py:25
  10.2 5.4 %collective-permute-start.5 = (s32[16,32]{1,0:T(8,128)S(1)}, s32[16,32]{1,0:T(8,128)S(1)}, u32[]{:S(2)}, u32[]{:S(2)}) collective-permute-start(s32[16,32]{1,0:T(8,128)S(1)} %shard_map.87.refs_0_), channel_id=1, source_target_pairs={{0,24},{2,26},{4,28},{6,30},{8,16},{10,18},{12,20},{14,22},{16,8},... | collective-permute-start | bytes 6152 | tf_op jit(solution)/shard_map/ppermute | solution.py:25
  17.1 13.4 %collective-permute-start.6 = (bf16[64,4096]{1,0:T(8,128)(2,1)S(1)}, bf16[64,4096]{1,0:T(8,128)(2,1)S(1)}, u32[]{:S(2)}, u32[]{:S(2)}) collective-permute-start(bf16[64,4096]{1,0:T(8,128)(2,1)S(1)} %get-tuple-element.33.refs_0_.refs_2_), channel_id=1, source_target_pairs={{0,1},{1,0},{2,3},{3,2},{4,5},{5,4},{6,7},{7,6},{8,9},{9,8},{10,11... | collective-permute-start | bytes 1572872 | tf_op jit(solution)/shard_map/ppermute | solution.py:25
  18.7 5.4 %collective-permute-start.9 = (bf16[16,4096]{1,0:T(8,128)(2,1)S(1)}, bf16[16,4096]{1,0:T(8,128)(2,1)S(1)}, u32[]{:S(2)}, u32[]{:S(2)}) collective-permute-start(bf16[16,4096]{1,0:T(8,128)(2,1)S(1)} %shard_map.89.refs_4_), channel_id=1, source_target_pairs={{0,8},{2,10},{4,12},{6,14},{8,0},{10,2},{12,4},{14,6},{16,24},{18,... | collective-permute-start | bytes 393224 | tf_op jit(solution)/shard_map/ppermute | solution.py:25
  18.8 11.7 %collective-permute-start.7 = (bf16[16,4096]{1,0:T(8,128)(2,1)S(1)}, bf16[16,4096]{1,0:T(8,128)(2,1)S(1)}, u32[]{:S(2)}, u32[]{:S(2)}) collective-permute-start(bf16[16,4096]{1,0:T(8,128)(2,1)S(1)} %get-tuple-element.34), channel_id=1, source_target_pairs={{0,20},{2,22},{4,16},{6,18},{8,28},{10,30},{12,24},{14,26},{16,4},... | collective-permute-start | bytes 393224 | tf_op jit(solution)/shard_map/ppermute | solution.py:25
  20.6 9.9 %collective-permute-start.8 = (bf16[16,4096]{1,0:T(8,128)(2,1)S(1)}, bf16[16,4096]{1,0:T(8,128)(2,1)S(1)}, u32[]{:S(2)}, u32[]{:S(2)}) collective-permute-start(bf16[16,4096]{1,0:T(8,128)(2,1)S(1)} %get-tuple-element.35), channel_id=1, source_target_pairs={{0,28},{2,30},{4,24},{6,26},{8,20},{10,22},{12,16},{14,18},{16,12}... | collective-permute-start | bytes 393224 | tf_op jit(solution)/shard_map/ppermute | solution.py:25
  30.6 14.5 %collective-permute-start.12 = (bf16[64,4096]{1,0:T(8,128)(2,1)S(1)}, bf16[64,4096]{1,0:T(8,128)(2,1)S(1)}, u32[]{:S(2)}, u32[]{:S(2)}) collective-permute-start(bf16[64,4096]{1,0:T(8,128)(2,1)S(1)} %get-tuple-element.38.refs_2_), channel_id=1, source_target_pairs={{0,4},{2,6},{4,0},{6,2},{8,12},{10,14},{12,8},{14,10},{16,20},{18,... | collective-permute-start | bytes 1572872 | tf_op jit(solution)/shard_map/ppermute | solution.py:25
  32.1 13.0 %collective-permute-start.13 = (bf16[32,4096]{1,0:T(8,128)(2,1)S(1)}, bf16[32,4096]{1,0:T(8,128)(2,1)S(1)}, u32[]{:S(2)}, u32[]{:S(2)}) collective-permute-start(bf16[32,4096]{1,0:T(8,128)(2,1)S(1)} %get-tuple-element.41), channel_id=1, source_target_pairs={{0,8},{2,10},{4,12},{6,14},{8,0},{10,2},{12,4},{14,6},{16,24},{18,... | collective-permute-start | bytes 786440 | tf_op jit(solution)/shard_map/ppermute | solution.py:25
  34.0 11.1 %collective-permute-start.14 = (bf16[32,4096]{1,0:T(8,128)(2,1)S(1)}, bf16[32,4096]{1,0:T(8,128)(2,1)S(1)}, u32[]{:S(2)}, u32[]{:S(2)}) collective-permute-start(bf16[32,4096]{1,0:T(8,128)(2,1)S(1)} %get-tuple-element.42.refs_6_), channel_id=1, source_target_pairs={{0,1},{1,0},{2,3},{3,2},{4,5},{5,4},{6,7},{7,6},{8,9},{9,8},{10,11... | collective-permute-start | bytes 786440 | tf_op jit(solution)/shard_map/ppermute | solution.py:25
  34.5 7.3 %collective-permute-start.10 = (bf16[16,4096]{1,0:T(8,128)(2,1)S(1)}, bf16[16,4096]{1,0:T(8,128)(2,1)S(1)}, u32[]{:S(2)}, u32[]{:S(2)}) collective-permute-start(bf16[16,4096]{1,0:T(8,128)(2,1)S(1)} %get-tuple-element.39), channel_id=1, source_target_pairs={{0,16},{2,18},{4,20},{6,22},{8,24},{10,26},{12,28},{14,30},{16,0},... | collective-permute-start | bytes 393224 | tf_op jit(solution)/shard_map/ppermute | solution.py:25
  34.5 10.6 %collective-permute-start.11 = (bf16[16,4096]{1,0:T(8,128)(2,1)S(1)}, bf16[16,4096]{1,0:T(8,128)(2,1)S(1)}, u32[]{:S(2)}, u32[]{:S(2)}) collective-permute-start(bf16[16,4096]{1,0:T(8,128)(2,1)S(1)} %get-tuple-element.40), channel_id=1, source_target_pairs={{0,24},{2,26},{4,28},{6,30},{8,16},{10,18},{12,20},{14,22},{16,8},... | collective-permute-start | bytes 393224 | tf_op jit(solution)/shard_map/ppermute | solution.py:25
  45.2 7.3 %collective-permute-start.15 = (bf16[32,4096]{1,0:T(8,128)(2,1)S(1)}, bf16[32,4096]{1,0:T(8,128)(2,1)S(1)}, u32[]{:S(2)}, u32[]{:S(2)}) collective-permute-start(bf16[32,4096]{1,0:T(8,128)(2,1)S(1)} %get-tuple-element.47), channel_id=1, source_target_pairs={{0,12},{2,14},{4,8},{6,10},{8,4},{10,6},{12,0},{14,2},{16,28},{18,... | collective-permute-start | bytes 786440 | tf_op jit(solution)/shard_map/ppermute | solution.py:25
  46.7 6.4 %collective-permute-start.16 = (bf16[32,4096]{1,0:T(8,128)(2,1)S(1)}, bf16[32,4096]{1,0:T(8,128)(2,1)S(1)}, u32[]{:S(2)}, u32[]{:S(2)}) collective-permute-start(bf16[32,4096]{1,0:T(8,128)(2,1)S(1)} %get-tuple-element.45.refs_8_), channel_id=1, source_target_pairs={{0,1},{1,0},{2,3},{3,2},{4,5},{5,4},{6,7},{7,6},{8,9},{9,8},{10,11... | collective-permute-start | bytes 786440 | tf_op jit(solution)/shard_map/ppermute | solution.py:25
  48.2 4.9 %collective-permute-start.17 = (bf16[32,4096]{1,0:T(8,128)(2,1)S(1)}, bf16[32,4096]{1,0:T(8,128)(2,1)S(1)}, u32[]{:S(2)}, u32[]{:S(2)}) collective-permute-start(bf16[32,4096]{1,0:T(8,128)(2,1)S(1)} %get-tuple-element.43.refs_0_), channel_id=1, source_target_pairs={{0,2},{2,0},{4,6},{6,4},{8,10},{10,8},{12,14},{14,12},{16,18},{18,... | collective-permute-start | bytes 786440 | tf_op jit(solution)/shard_map/ppermute | solution.py:25
  48.2 4.9 %collective-permute-start.18 = (bf16[32,4096]{1,0:T(8,128)(2,1)S(1)}, bf16[32,4096]{1,0:T(8,128)(2,1)S(1)}, u32[]{:S(2)}, u32[]{:S(2)}) collective-permute-start(bf16[32,4096]{1,0:T(8,128)(2,1)S(1)} %get-tuple-element.44.refs_1_), channel_id=1, source_target_pairs={{0,2},{2,0},{4,6},{6,4},{8,10},{10,8},{12,14},{14,12},{16,18},{18,... | collective-permute-start | bytes 786440 | tf_op jit(solution)/shard_map/ppermute | solution.py:25
  58.5 12.8 %collective-permute-start.20 = (f32[32,2176]{1,0:T(8,128)S(1)}, f32[32,2176]{1,0:T(8,128)S(1)}, u32[]{:S(2)}, u32[]{:S(2)}) collective-permute-start(f32[32,2176]{1,0:T(8,128)S(1)} %get-tuple-element.55), channel_id=1, source_target_pairs={{0,4},{1,5},{2,6},{3,7},{4,0},{5,1},{6,2},{7,3},{8,12},{9,13},{10,... | collective-permute-start | bytes 835592 | tf_op jit(solution)/shard_map/ppermute | solution.py:25
  60.0 11.4 %collective-permute-start.21 = (f32[32,2176]{1,0:T(8,128)S(1)}, f32[32,2176]{1,0:T(8,128)S(1)}, u32[]{:S(2)}, u32[]{:S(2)}) collective-permute-start(f32[32,2176]{1,0:T(8,128)S(1)} %get-tuple-element.56), channel_id=1, source_target_pairs={{0,1},{1,0},{2,3},{3,2},{4,5},{5,4},{6,7},{7,6},{8,9},{9,8},{10,11... | collective-permute-start | bytes 835592 | tf_op jit(solution)/shard_map/ppermute | solution.py:25
  61.4 9.9 %collective-permute-start.22 = (bf16[32,2176]{1,0:T(8,128)(2,1)S(1)}, bf16[32,2176]{1,0:T(8,128)(2,1)S(1)}, u32[]{:S(2)}, u32[]{:S(2)}) collective-permute-start(bf16[32,2176]{1,0:T(8,128)(2,1)S(1)} %get-tuple-element.57), channel_id=1, source_target_pairs={{0,5},{1,4},{2,7},{3,6},{4,1},{5,0},{6,3},{7,2},{8,13},{9,12},{10,... | collective-permute-start | bytes 417800 | tf_op jit(solution)/shard_map/ppermute | solution.py:25
  71.5 8.2 %collective-permute-start.23 = (f32[8,2176]{1,0:T(8,128)S(1)}, f32[8,2176]{1,0:T(8,128)S(1)}, u32[]{:S(2)}, u32[]{:S(2)}) collective-permute-start(f32[8,2176]{1,0:T(8,128)S(1)} %get-tuple-element.60), channel_id=1, source_target_pairs={{0,16},{2,18},{4,20},{6,22},{8,24},{10,26},{12,28},{14,30},{16,0},... | collective-permute-start | bytes 208904 | tf_op jit(solution)/shard_map/ppermute | solution.py:25
  72.8 6.9 %collective-permute-start.24 = (f32[8,2176]{1,0:T(8,128)S(1)}, f32[8,2176]{1,0:T(8,128)S(1)}, u32[]{:S(2)}, u32[]{:S(2)}) collective-permute-start(f32[8,2176]{1,0:T(8,128)S(1)} %get-tuple-element.61), channel_id=1, source_target_pairs={{0,8},{2,10},{4,12},{6,14},{8,0},{10,2},{12,4},{14,6},{16,24},{18,... | collective-permute-start | bytes 208904 | tf_op jit(solution)/shard_map/ppermute | solution.py:25
  74.0 5.7 %collective-permute-start.25 = (bf16[8,2176]{1,0:T(8,128)(2,1)S(1)}, bf16[8,2176]{1,0:T(8,128)(2,1)S(1)}, u32[]{:S(2)}, u32[]{:S(2)}) collective-permute-start(bf16[8,2176]{1,0:T(8,128)(2,1)S(1)} %get-tuple-element.62), channel_id=1, source_target_pairs={{0,24},{2,26},{4,28},{6,30},{8,16},{10,18},{12,20},{14,22},{16,8},... | collective-permute-start | bytes 104456 | tf_op jit(solution)/shard_map/ppermute | solution.py:25
  (9 other events, 47.5 us)

commit v2 on v1

--- a/solution.py
+++ b/solution.py
@@ -402,7 +402,10 @@
     second = jax.ShapeDtypeStruct((block, part), jnp.float32)
     total, *going = pl.pallas_call(
         second_sum,
-        out_shape=[second] * (rest - 1) + [jax.ShapeDtypeStruct(second.shape, jnp.bfloat16)],
+        out_shape=[
+            jax.ShapeDtypeStruct(second.shape, jnp.bfloat16 if i == 1 else jnp.float32)
+            for i in range(rest)
+        ],
         in_specs=[WHOLE] * 5,
         out_specs=[WHOLE] * rest,
         compiler_params=budget(payload, payload),
@@ -410,7 +413,7 @@
             flops=4 * first.size, bytes_accessed=20 * first.size, transcendentals=0
         ),
     )(own, *came, done)
-    for value, order in zip(going, orders[1:rest]):
+    for value, order in reversed(list(zip(going, orders[1:rest]))):
         total = total + exchange(value, ("loop",), order).astype(jnp.float32)
     mean_loss = (total[0, half] + total[0, half + LOSS // 2]) / (count * loop * reps)
     total = total[:, :half]

time: 86.1 us -> 85.2 us (0.990)
  transfers between devices with their start and end apart: 27 -> 27, of which waited for: 11 -> 12; matrix products, arithmetic and copies ran while one was open for 1% -> 1% of each run, Pallas kernels for 6% -> 6%
where the time goes in v2:
time: 85.2 us; the launch traced here: 85 us
  starting transfers between devices  36.6 us (43%)
  waiting for transfers between devices  32 us (38%)
  Pallas kernels  9.59 us (11%)
  between operations  3.22 us (4%)
  local copies, waits for them, and re-layouts  2.88 us (3%)
    ppermute x27, starting transfers between devices, exchange(): return lax.ppermute(value, axes, [(i, i ^ mask) for i in range(size)])  36.6 us
    ppermute x27, waiting for transfers between devices, exchange(): return lax.ppermute(value, axes, [(i, i ^ mask) for i in range(size)])  32 us
    pallas_call x1, Pallas kernels, shards(): pl.pallas_call(grad_kernel, out_shape=[jax.ShapeDtypeStruct((count, width...  3.28 us
    pallas_call x1, Pallas kernels, shards(): pl.pallas_call(functools.partial(score_kernel, last_counts, len(other_pai...  2.45 us
    unnamed x12, local copies, waits for them, and re-layouts  2.29 us
  transfers between devices with their start and end apart: 27, of which 12 were waited for; matrix products, arithmetic and copies ran while one was open for 1% of the time, Pallas kernels for 6%

profile of v2, /device:TPU:0, one launch (start us, length us, event | category | flops | bytes accessed | tf_op | source)
XLA Modules:
  0.0 85.0 jit_solution(1022803127579412909)
XLA Ops:
  1.1 2.6 %collective-permute-start.2 = (s32[8,32]{1,0:T(8,128)}, s32[8,32]{1,0:T(8,128)S(1)}, u32[]{:S(2)}, u32[]{:S(2)}) collective-permute-start(s32[8,32]{1,0:T(8,128)} %bitcast.7), channel_id=1, source_target_pairs={{0,4},{2,6},{4,0},{6,2},{8,12},{10,14},{12,8},{14,10},{16,20},{18,... | collective-permute-start | bytes 3080 | tf_op jit(solution)/shard_map/ppermute | solution.py:25
  3.7 2.6 %collective-permute-start.1 = (bf16[8,4096]{1,0:T(8,128)(2,1)}, bf16[8,4096]{1,0:T(8,128)(2,1)S(1)}, u32[]{:S(2)}, u32[]{:S(2)}) collective-permute-start(bf16[8,4096]{1,0:T(8,128)(2,1)} %refs_0_.3), channel_id=1, source_target_pairs={{0,16},{2,18},{4,20},{6,22},{8,24},{10,26},{12,28},{14,30},{16,0},... | collective-permute-start | bytes 196616 | tf_op jit(solution)/shard_map/ppermute | solution.py:25
  7.0 1.6 %collective-permute-start.3 = (s32[16,32]{1,0:T(8,128)S(1)}, s32[16,32]{1,0:T(8,128)S(1)}, u32[]{:S(2)}, u32[]{:S(2)}) collective-permute-start(s32[16,32]{1,0:T(8,128)S(1)} %shard_map.87.refs_0_), channel_id=1, source_target_pairs={{0,8},{2,10},{4,12},{6,14},{8,0},{10,2},{12,4},{14,6},{16,24},{18,... | collective-permute-start | bytes 6152 | tf_op jit(solution)/shard_map/ppermute | solution.py:25
  8.6 1.6 %collective-permute-start.4 = (s32[16,32]{1,0:T(8,128)S(1)}, s32[16,32]{1,0:T(8,128)S(1)}, u32[]{:S(2)}, u32[]{:S(2)}) collective-permute-start(s32[16,32]{1,0:T(8,128)S(1)} %shard_map.87.refs_0_), channel_id=1, source_target_pairs={{0,16},{2,18},{4,20},{6,22},{8,24},{10,26},{12,28},{14,30},{16,0},... | collective-permute-start | bytes 6152 | tf_op jit(solution)/shard_map/ppermute | solution.py:25
  11.5 1.6 %copy-done.1 = bf16[256,4096]{1,0:T(8,128)(2,1)S(1)} copy-done((bf16[256,4096]{1,0:T(8,128)(2,1)S(1)}, bf16[256,4096]{1,0:T(8,128)(2,1)}, u32[]{:S(2)}) %copy-start.1) | copy-done | bytes 2097176
  13.3 2.4 %collective-permute-done.5.refs_3_ = s32[16,32]{1,0:T(8,128)S(1)} collective-permute-done((s32[16,32]{1,0:T(8,128)S(1)}, s32[16,32]{1,0:T(8,128)S(1)}, u32[]{:S(2)}, u32[]{:S(2)}) %collective-permute-start.5) | collective-permute-done | bytes 2080 | tf_op jit(solution)/shard_map/ppermute | solution.py:25
  17.1 1.6 %collective-permute-start.6 = (bf16[64,4096]{1,0:T(8,128)(2,1)S(1)}, bf16[64,4096]{1,0:T(8,128)(2,1)S(1)}, u32[]{:S(2)}, u32[]{:S(2)}) collective-permute-start(bf16[64,4096]{1,0:T(8,128)(2,1)S(1)} %get-tuple-element.33.refs_0_.refs_2_), channel_id=1, source_target_pairs={{0,1},{1,0},{2,3},{3,2},{4,5},{5,4},{6,7},{7,6},{8,9},{9,8},{10,11... | collective-permute-start | bytes 1572872 | tf_op jit(solution)/shard_map/ppermute | solution.py:25
  18.8 1.8 %collective-permute-start.7 = (bf16[16,4096]{1,0:T(8,128)(2,1)S(1)}, bf16[16,4096]{1,0:T(8,128)(2,1)S(1)}, u32[]{:S(2)}, u32[]{:S(2)}) collective-permute-start(bf16[16,4096]{1,0:T(8,128)(2,1)S(1)} %get-tuple-element.34), channel_id=1, source_target_pairs={{0,20},{2,22},{4,16},{6,18},{8,28},{10,30},{12,24},{14,26},{16,4},... | collective-permute-start | bytes 393224 | tf_op jit(solution)/shard_map/ppermute | solution.py:25
  20.6 3.5 %collective-permute-start.8 = (bf16[16,4096]{1,0:T(8,128)(2,1)S(1)}, bf16[16,4096]{1,0:T(8,128)(2,1)S(1)}, u32[]{:S(2)}, u32[]{:S(2)}) collective-permute-start(bf16[16,4096]{1,0:T(8,128)(2,1)S(1)} %get-tuple-element.35), channel_id=1, source_target_pairs={{0,28},{2,30},{4,24},{6,26},{8,20},{10,22},{12,16},{14,18},{16,12}... | collective-permute-start | bytes 393224 | tf_op jit(solution)/shard_map/ppermute | solution.py:25
  24.1 6.4 %collective-permute-done.7.refs_2_ = bf16[16,4096]{1,0:T(8,128)(2,1)S(1)} collective-permute-done((bf16[16,4096]{1,0:T(8,128)(2,1)S(1)}, bf16[16,4096]{1,0:T(8,128)(2,1)S(1)}, u32[]{:S(2)}, u32[]{:S(2)}) %collective-permute-start.7) | collective-permute-done | bytes 131104 | tf_op jit(solution)/shard_map/ppermute | solution.py:25
  30.6 1.5 %collective-permute-start.12 = (bf16[64,4096]{1,0:T(8,128)(2,1)S(1)}, bf16[64,4096]{1,0:T(8,128)(2,1)S(1)}, u32[]{:S(2)}, u32[]{:S(2)}) collective-permute-start(bf16[64,4096]{1,0:T(8,128)(2,1)S(1)} %get-tuple-element.38.refs_2_), channel_id=1, source_target_pairs={{0,4},{2,6},{4,0},{6,2},{8,12},{10,14},{12,8},{14,10},{16,20},{18,... | collective-permute-start | bytes 1572872 | tf_op jit(solution)/shard_map/ppermute | solution.py:25
  32.1 1.9 %collective-permute-start.13 = (bf16[32,4096]{1,0:T(8,128)(2,1)S(1)}, bf16[32,4096]{1,0:T(8,128)(2,1)S(1)}, u32[]{:S(2)}, u32[]{:S(2)}) collective-permute-start(bf16[32,4096]{1,0:T(8,128)(2,1)S(1)} %get-tuple-element.41), channel_id=1, source_target_pairs={{0,8},{2,10},{4,12},{6,14},{8,0},{10,2},{12,4},{14,6},{16,24},{18,... | collective-permute-start | bytes 786440 | tf_op jit(solution)/shard_map/ppermute | solution.py:25
  34.5 2.5 %collective-permute-start.11 = (bf16[16,4096]{1,0:T(8,128)(2,1)S(1)}, bf16[16,4096]{1,0:T(8,128)(2,1)S(1)}, u32[]{:S(2)}, u32[]{:S(2)}) collective-permute-start(bf16[16,4096]{1,0:T(8,128)(2,1)S(1)} %get-tuple-element.40), channel_id=1, source_target_pairs={{0,24},{2,26},{4,28},{6,30},{8,16},{10,18},{12,20},{14,22},{16,8},... | collective-permute-start | bytes 393224 | tf_op jit(solution)/shard_map/ppermute | solution.py:25
  37.1 4.7 %collective-permute-done.10.refs_3_ = bf16[16,4096]{1,0:T(8,128)(2,1)S(1)} collective-permute-done((bf16[16,4096]{1,0:T(8,128)(2,1)S(1)}, bf16[16,4096]{1,0:T(8,128)(2,1)S(1)}, u32[]{:S(2)}, u32[]{:S(2)}) %collective-permute-start.10) | collective-permute-done | bytes 131104 | tf_op jit(solution)/shard_map/ppermute | solution.py:25
  41.8 3.3 %collective-permute-done.11.refs_4_ = bf16[16,4096]{1,0:T(8,128)(2,1)S(1)} collective-permute-done((bf16[16,4096]{1,0:T(8,128)(2,1)S(1)}, bf16[16,4096]{1,0:T(8,128)(2,1)S(1)}, u32[]{:S(2)}, u32[]{:S(2)}) %collective-permute-start.11) | collective-permute-done | bytes 131104 | tf_op jit(solution)/shard_map/ppermute | solution.py:25
  49.5 3.0 %collective-permute-done.15.refs_0_ = bf16[32,4096]{1,0:T(8,128)(2,1)S(1)} collective-permute-done((bf16[32,4096]{1,0:T(8,128)(2,1)S(1)}, bf16[32,4096]{1,0:T(8,128)(2,1)S(1)}, u32[]{:S(2)}, u32[]{:S(2)}) %collective-permute-start.15) | collective-permute-done | bytes 262176 | tf_op jit(solution)/shard_map/ppermute | solution.py:25
  53.1 2.5 %shard_map.93 = (bf16[256,256]{1,0:T(8,128)(2,1)S(1)}, bf16[256,128]{1,0:T(8,128)(2,1)S(1)}, bf16[128,4096]{1,0:T(8,128)(2,1)S(1)}, f32[64,4352]{1,0:T(8,128)S(1)}) custom-call(s32[2]{0:T(128)S(1)} %pad_add_fusion.meta, s32[1,32]{1,0:T(1,128)S(1)} %copy-done.5, bf16[256,4096]{1,0:T(8,128)(2,1)S(1)} %copy-done, s32[1,256]{1,0:T(1,128)S(1)} %bitcast.9, ...), custom_call_target="tpu_custom_call" | custom-call | flops 411041792 | bytes 5308416 | tf_op jit(solution)/shard_map/pallas_call | solution.py:340
  56.7 1.7 %collective-permute-done.19.sent = f32[64,4352]{1,0:T(8,128)S(1)} collective-permute-done((f32[64,4352]{1,0:T(8,128)S(1)}, f32[64,4352]{1,0:T(8,128)S(1)}, u32[]{:S(2)}, u32[]{:S(2)}) %collective-permute-start.19) | collective-permute-done | bytes 1114144 | tf_op jit(solution)/shard_map/ppermute | solution.py:25
  58.5 1.5 %collective-permute-start.20 = (f32[32,2176]{1,0:T(8,128)S(1)}, f32[32,2176]{1,0:T(8,128)S(1)}, u32[]{:S(2)}, u32[]{:S(2)}) collective-permute-start(f32[32,2176]{1,0:T(8,128)S(1)} %get-tuple-element.55), channel_id=1, source_target_pairs={{0,4},{1,5},{2,6},{3,7},{4,0},{5,1},{6,2},{7,3},{8,12},{9,13},{10,... | collective-permute-start | bytes 835592 | tf_op jit(solution)/shard_map/ppermute | solution.py:25
  62.0 3.3 %shard_map.94 = (f32[256,4096]{1,0:T(8,128)}, f32[8,128]{1,0:T(8,128)S(1)}) custom-call(bf16[256,256]{1,0:T(8,128)(2,1)S(1)} %get-tuple-element.48.weights_1.weights, bf16[256,128]{1,0:T(8,128)(2,1)S(1)} %get-tuple-element.49.weights_2, bf16[256,4096]{1,0:T(8,128)(2,1)S(1)} %get-tuple-element.50.rows_1, bf16[128,4096]{1,0:T(8,128)(2,1)S(1)} %get-tuple-element.51.rows_2), custom_call_target="tpu_custom_call" | custom-call | flops 805306368 | bytes 7340032 | tf_op jit(solution)/shard_map/pallas_call | solution.py:372
  65.3 6.0 %collective-permute-done.22.from_xy = bf16[32,2176]{1,0:T(8,128)(2,1)S(1)} collective-permute-done((bf16[32,2176]{1,0:T(8,128)(2,1)S(1)}, bf16[32,2176]{1,0:T(8,128)(2,1)S(1)}, u32[]{:S(2)}, u32[]{:S(2)}) %collective-permute-start.22) | collective-permute-done | bytes 139296 | tf_op jit(solution)/shard_map/ppermute | solution.py:25
  71.5 1.8 %collective-permute-start.23 = (f32[8,2176]{1,0:T(8,128)S(1)}, f32[8,2176]{1,0:T(8,128)S(1)}, u32[]{:S(2)}, u32[]{:S(2)}) collective-permute-start(f32[8,2176]{1,0:T(8,128)S(1)} %get-tuple-element.60), channel_id=1, source_target_pairs={{0,24},{2,26},{4,28},{6,30},{8,16},{10,18},{12,20},{14,22},{16,8},... | collective-permute-start | bytes 208904 | tf_op jit(solution)/shard_map/ppermute | solution.py:25
  73.4 2.6 %collective-permute-start.25 = (bf16[8,2176]{1,0:T(8,128)(2,1)S(1)}, bf16[8,2176]{1,0:T(8,128)(2,1)S(1)}, u32[]{:S(2)}, u32[]{:S(2)}) collective-permute-start(bf16[8,2176]{1,0:T(8,128)(2,1)S(1)} %get-tuple-element.62), channel_id=1, source_target_pairs={{0,16},{2,18},{4,20},{6,22},{8,24},{10,26},{12,28},{14,30},{16,0},... | collective-permute-start | bytes 104456 | tf_op jit(solution)/shard_map/ppermute | solution.py:25
  76.0 2.5 %collective-permute-done.25 = bf16[8,2176]{1,0:T(8,128)(2,1)S(1)} collective-permute-done((bf16[8,2176]{1,0:T(8,128)(2,1)S(1)}, bf16[8,2176]{1,0:T(8,128)(2,1)S(1)}, u32[]{:S(2)}, u32[]{:S(2)}) %collective-permute-start.25) | collective-permute-done | bytes 34848 | tf_op jit(solution)/shard_map/ppermute | solution.py:25
  (60 shorter events, 17.3 us)
Async XLA Ops:
  0.6 15.0 %collective-permute-start = (bf16[256,4096]{1,0:T(8,128)(2,1)}, bf16[256,4096]{1,0:T(8,128)(2,1)S(1)}, u32[]{:S(2)}, u32[]{:S(2)}) collective-permute-start(bf16[256,4096]{1,0:T(8,128)(2,1)} %refs_0_.2), channel_id=1, source_target_pairs={{0,2},{2,0},{4,6},{6,4},{8,10},{10,8},{12,14},{14,12},{16,18},{18,... | collective-permute-start | bytes 6291464 | tf_op jit(solution)/shard_map/ppermute | solution.py:25
  1.1 5.8 %collective-permute-start.2 = (s32[8,32]{1,0:T(8,128)}, s32[8,32]{1,0:T(8,128)S(1)}, u32[]{:S(2)}, u32[]{:S(2)}) collective-permute-start(s32[8,32]{1,0:T(8,128)} %bitcast.7), channel_id=1, source_target_pairs={{0,4},{2,6},{4,0},{6,2},{8,12},{10,14},{12,8},{14,10},{16,20},{18,... | collective-permute-start | bytes 3080 | tf_op jit(solution)/shard_map/ppermute | solution.py:25
  3.7 11.9 %collective-permute-start.1 = (bf16[8,4096]{1,0:T(8,128)(2,1)}, bf16[8,4096]{1,0:T(8,128)(2,1)S(1)}, u32[]{:S(2)}, u32[]{:S(2)}) collective-permute-start(bf16[8,4096]{1,0:T(8,128)(2,1)} %refs_0_.3), channel_id=1, source_target_pairs={{0,16},{2,18},{4,20},{6,22},{8,24},{10,26},{12,28},{14,30},{16,0},... | collective-permute-start | bytes 196616 | tf_op jit(solution)/shard_map/ppermute | solution.py:25
  7.0 6.3 %collective-permute-start.3 = (s32[16,32]{1,0:T(8,128)S(1)}, s32[16,32]{1,0:T(8,128)S(1)}, u32[]{:S(2)}, u32[]{:S(2)}) collective-permute-start(s32[16,32]{1,0:T(8,128)S(1)} %shard_map.87.refs_0_), channel_id=1, source_target_pairs={{0,8},{2,10},{4,12},{6,14},{8,0},{10,2},{12,4},{14,6},{16,24},{18,... | collective-permute-start | bytes 6152 | tf_op jit(solution)/shard_map/ppermute | solution.py:25
  10.2 5.4 %collective-permute-start.5 = (s32[16,32]{1,0:T(8,128)S(1)}, s32[16,32]{1,0:T(8,128)S(1)}, u32[]{:S(2)}, u32[]{:S(2)}) collective-permute-start(s32[16,32]{1,0:T(8,128)S(1)} %shard_map.87.refs_0_), channel_id=1, source_target_pairs={{0,24},{2,26},{4,28},{6,30},{8,16},{10,18},{12,20},{14,22},{16,8},... | collective-permute-start | bytes 6152 | tf_op jit(solution)/shard_map/ppermute | solution.py:25
  17.1 13.4 %collective-permute-start.6 = (bf16[64,4096]{1,0:T(8,128)(2,1)S(1)}, bf16[64,4096]{1,0:T(8,128)(2,1)S(1)}, u32[]{:S(2)}, u32[]{:S(2)}) collective-permute-start(bf16[64,4096]{1,0:T(8,128)(2,1)S(1)} %get-tuple-element.33.refs_0_.refs_2_), channel_id=1, source_target_pairs={{0,1},{1,0},{2,3},{3,2},{4,5},{5,4},{6,7},{7,6},{8,9},{9,8},{10,11... | collective-permute-start | bytes 1572872 | tf_op jit(solution)/shard_map/ppermute | solution.py:25
  18.7 5.4 %collective-permute-start.9 = (bf16[16,4096]{1,0:T(8,128)(2,1)S(1)}, bf16[16,4096]{1,0:T(8,128)(2,1)S(1)}, u32[]{:S(2)}, u32[]{:S(2)}) collective-permute-start(bf16[16,4096]{1,0:T(8,128)(2,1)S(1)} %shard_map.89.refs_4_), channel_id=1, source_target_pairs={{0,8},{2,10},{4,12},{6,14},{8,0},{10,2},{12,4},{14,6},{16,24},{18,... | collective-permute-start | bytes 393224 | tf_op jit(solution)/shard_map/ppermute | solution.py:25
  18.8 11.7 %collective-permute-start.7 = (bf16[16,4096]{1,0:T(8,128)(2,1)S(1)}, bf16[16,4096]{1,0:T(8,128)(2,1)S(1)}, u32[]{:S(2)}, u32[]{:S(2)}) collective-permute-start(bf16[16,4096]{1,0:T(8,128)(2,1)S(1)} %get-tuple-element.34), channel_id=1, source_target_pairs={{0,20},{2,22},{4,16},{6,18},{8,28},{10,30},{12,24},{14,26},{16,4},... | collective-permute-start | bytes 393224 | tf_op jit(solution)/shard_map/ppermute | solution.py:25
  20.6 9.9 %collective-permute-start.8 = (bf16[16,4096]{1,0:T(8,128)(2,1)S(1)}, bf16[16,4096]{1,0:T(8,128)(2,1)S(1)}, u32[]{:S(2)}, u32[]{:S(2)}) collective-permute-start(bf16[16,4096]{1,0:T(8,128)(2,1)S(1)} %get-tuple-element.35), channel_id=1, source_target_pairs={{0,28},{2,30},{4,24},{6,26},{8,20},{10,22},{12,16},{14,18},{16,12}... | collective-permute-start | bytes 393224 | tf_op jit(solution)/shard_map/ppermute | solution.py:25
  30.6 14.5 %collective-permute-start.12 = (bf16[64,4096]{1,0:T(8,128)(2,1)S(1)}, bf16[64,4096]{1,0:T(8,128)(2,1)S(1)}, u32[]{:S(2)}, u32[]{:S(2)}) collective-permute-start(bf16[64,4096]{1,0:T(8,128)(2,1)S(1)} %get-tuple-element.38.refs_2_), channel_id=1, source_target_pairs={{0,4},{2,6},{4,0},{6,2},{8,12},{10,14},{12,8},{14,10},{16,20},{18,... | collective-permute-start | bytes 1572872 | tf_op jit(solution)/shard_map/ppermute | solution.py:25
  32.1 13.0 %collective-permute-start.13 = (bf16[32,4096]{1,0:T(8,128)(2,1)S(1)}, bf16[32,4096]{1,0:T(8,128)(2,1)S(1)}, u32[]{:S(2)}, u32[]{:S(2)}) collective-permute-start(bf16[32,4096]{1,0:T(8,128)(2,1)S(1)} %get-tuple-element.41), channel_id=1, source_target_pairs={{0,8},{2,10},{4,12},{6,14},{8,0},{10,2},{12,4},{14,6},{16,24},{18,... | collective-permute-start | bytes 786440 | tf_op jit(solution)/shard_map/ppermute | solution.py:25
  34.0 11.1 %collective-permute-start.14 = (bf16[32,4096]{1,0:T(8,128)(2,1)S(1)}, bf16[32,4096]{1,0:T(8,128)(2,1)S(1)}, u32[]{:S(2)}, u32[]{:S(2)}) collective-permute-start(bf16[32,4096]{1,0:T(8,128)(2,1)S(1)} %get-tuple-element.42.refs_6_), channel_id=1, source_target_pairs={{0,1},{1,0},{2,3},{3,2},{4,5},{5,4},{6,7},{7,6},{8,9},{9,8},{10,11... | collective-permute-start | bytes 786440 | tf_op jit(solution)/shard_map/ppermute | solution.py:25
  34.5 7.3 %collective-permute-start.10 = (bf16[16,4096]{1,0:T(8,128)(2,1)S(1)}, bf16[16,4096]{1,0:T(8,128)(2,1)S(1)}, u32[]{:S(2)}, u32[]{:S(2)}) collective-permute-start(bf16[16,4096]{1,0:T(8,128)(2,1)S(1)} %get-tuple-element.39), channel_id=1, source_target_pairs={{0,16},{2,18},{4,20},{6,22},{8,24},{10,26},{12,28},{14,30},{16,0},... | collective-permute-start | bytes 393224 | tf_op jit(solution)/shard_map/ppermute | solution.py:25
  34.5 10.6 %collective-permute-start.11 = (bf16[16,4096]{1,0:T(8,128)(2,1)S(1)}, bf16[16,4096]{1,0:T(8,128)(2,1)S(1)}, u32[]{:S(2)}, u32[]{:S(2)}) collective-permute-start(bf16[16,4096]{1,0:T(8,128)(2,1)S(1)} %get-tuple-element.40), channel_id=1, source_target_pairs={{0,24},{2,26},{4,28},{6,30},{8,16},{10,18},{12,20},{14,22},{16,8},... | collective-permute-start | bytes 393224 | tf_op jit(solution)/shard_map/ppermute | solution.py:25
  45.2 7.3 %collective-permute-start.15 = (bf16[32,4096]{1,0:T(8,128)(2,1)S(1)}, bf16[32,4096]{1,0:T(8,128)(2,1)S(1)}, u32[]{:S(2)}, u32[]{:S(2)}) collective-permute-start(bf16[32,4096]{1,0:T(8,128)(2,1)S(1)} %get-tuple-element.47), channel_id=1, source_target_pairs={{0,12},{2,14},{4,8},{6,10},{8,4},{10,6},{12,0},{14,2},{16,28},{18,... | collective-permute-start | bytes 786440 | tf_op jit(solution)/shard_map/ppermute | solution.py:25
  46.7 6.4 %collective-permute-start.16 = (bf16[32,4096]{1,0:T(8,128)(2,1)S(1)}, bf16[32,4096]{1,0:T(8,128)(2,1)S(1)}, u32[]{:S(2)}, u32[]{:S(2)}) collective-permute-start(bf16[32,4096]{1,0:T(8,128)(2,1)S(1)} %get-tuple-element.45.refs_8_), channel_id=1, source_target_pairs={{0,1},{1,0},{2,3},{3,2},{4,5},{5,4},{6,7},{7,6},{8,9},{9,8},{10,11... | collective-permute-start | bytes 786440 | tf_op jit(solution)/shard_map/ppermute | solution.py:25
  48.2 4.9 %collective-permute-start.17 = (bf16[32,4096]{1,0:T(8,128)(2,1)S(1)}, bf16[32,4096]{1,0:T(8,128)(2,1)S(1)}, u32[]{:S(2)}, u32[]{:S(2)}) collective-permute-start(bf16[32,4096]{1,0:T(8,128)(2,1)S(1)} %get-tuple-element.43.refs_0_), channel_id=1, source_target_pairs={{0,2},{2,0},{4,6},{6,4},{8,10},{10,8},{12,14},{14,12},{16,18},{18,... | collective-permute-start | bytes 786440 | tf_op jit(solution)/shard_map/ppermute | solution.py:25
  48.2 4.9 %collective-permute-start.18 = (bf16[32,4096]{1,0:T(8,128)(2,1)S(1)}, bf16[32,4096]{1,0:T(8,128)(2,1)S(1)}, u32[]{:S(2)}, u32[]{:S(2)}) collective-permute-start(bf16[32,4096]{1,0:T(8,128)(2,1)S(1)} %get-tuple-element.44.refs_1_), channel_id=1, source_target_pairs={{0,2},{2,0},{4,6},{6,4},{8,10},{10,8},{12,14},{14,12},{16,18},{18,... | collective-permute-start | bytes 786440 | tf_op jit(solution)/shard_map/ppermute | solution.py:25
  58.5 12.8 %collective-permute-start.20 = (f32[32,2176]{1,0:T(8,128)S(1)}, f32[32,2176]{1,0:T(8,128)S(1)}, u32[]{:S(2)}, u32[]{:S(2)}) collective-permute-start(f32[32,2176]{1,0:T(8,128)S(1)} %get-tuple-element.55), channel_id=1, source_target_pairs={{0,4},{1,5},{2,6},{3,7},{4,0},{5,1},{6,2},{7,3},{8,12},{9,13},{10,... | collective-permute-start | bytes 835592 | tf_op jit(solution)/shard_map/ppermute | solution.py:25
  60.0 11.4 %collective-permute-start.21 = (f32[32,2176]{1,0:T(8,128)S(1)}, f32[32,2176]{1,0:T(8,128)S(1)}, u32[]{:S(2)}, u32[]{:S(2)}) collective-permute-start(f32[32,2176]{1,0:T(8,128)S(1)} %get-tuple-element.56), channel_id=1, source_target_pairs={{0,1},{1,0},{2,3},{3,2},{4,5},{5,4},{6,7},{7,6},{8,9},{9,8},{10,11... | collective-permute-start | bytes 835592 | tf_op jit(solution)/shard_map/ppermute | solution.py:25
  61.4 9.9 %collective-permute-start.22 = (bf16[32,2176]{1,0:T(8,128)(2,1)S(1)}, bf16[32,2176]{1,0:T(8,128)(2,1)S(1)}, u32[]{:S(2)}, u32[]{:S(2)}) collective-permute-start(bf16[32,2176]{1,0:T(8,128)(2,1)S(1)} %get-tuple-element.57), channel_id=1, source_target_pairs={{0,5},{1,4},{2,7},{3,6},{4,1},{5,0},{6,3},{7,2},{8,13},{9,12},{10,... | collective-permute-start | bytes 417800 | tf_op jit(solution)/shard_map/ppermute | solution.py:25
  71.5 7.0 %collective-permute-start.23 = (f32[8,2176]{1,0:T(8,128)S(1)}, f32[8,2176]{1,0:T(8,128)S(1)}, u32[]{:S(2)}, u32[]{:S(2)}) collective-permute-start(f32[8,2176]{1,0:T(8,128)S(1)} %get-tuple-element.60), channel_id=1, source_target_pairs={{0,24},{2,26},{4,28},{6,30},{8,16},{10,18},{12,20},{14,22},{16,8},... | collective-permute-start | bytes 208904 | tf_op jit(solution)/shard_map/ppermute | solution.py:25
  73.4 5.4 %collective-permute-start.24 = (f32[8,2176]{1,0:T(8,128)S(1)}, f32[8,2176]{1,0:T(8,128)S(1)}, u32[]{:S(2)}, u32[]{:S(2)}) collective-permute-start(f32[8,2176]{1,0:T(8,128)S(1)} %get-tuple-element.61), channel_id=1, source_target_pairs={{0,8},{2,10},{4,12},{6,14},{8,0},{10,2},{12,4},{14,6},{16,24},{18,... | collective-permute-start | bytes 208904 | tf_op jit(solution)/shard_map/ppermute | solution.py:25
  73.4 5.1 %collective-permute-start.25 = (bf16[8,2176]{1,0:T(8,128)(2,1)S(1)}, bf16[8,2176]{1,0:T(8,128)(2,1)S(1)}, u32[]{:S(2)}, u32[]{:S(2)}) collective-permute-start(bf16[8,2176]{1,0:T(8,128)(2,1)S(1)} %get-tuple-element.62), channel_id=1, source_target_pairs={{0,16},{2,18},{4,20},{6,22},{8,24},{10,26},{12,28},{14,30},{16,0},... | collective-permute-start | bytes 104456 | tf_op jit(solution)/shard_map/ppermute | solution.py:25
  (9 other events, 47.5 us)

commit v3 on v2

--- a/solution.py
+++ b/solution.py
@@ -37,7 +37,7 @@
         picked = []
         for m in range(count + len(pieces)):
             at = m % 2 * slots
-            tile = asked[m // 2][at:at + slots, :]
+            tile = asked[-(m // 2)][at:at + slots, :]
             column = jnp.sum(jnp.where(lanes == owner, tile, 0), axis=1, keepdims=True)
             picked.append(jnp.where(column == rows, 1.0, 0.0))
         return jnp.concatenate(picked, axis=0).astype(jnp.bfloat16)
@@ -224,7 +224,7 @@
     wanted = jnp.transpose(hard_rows, (0, 2, 1)).reshape(slots, owners)
     neighbour, (own_wanted,) = exchange(wanted, ("loop",), 2), pack([[(0, 0, slots)]], wanted)
     asked, = pack([[(0, 0, slots), (1, 0, slots)]], own_wanted, neighbour)
-    asked = [asked] + [exchange(asked, ("loop",), 4 * k) for k in range(1, rest)]
+    asked = [asked] + [exchange(asked, ("loop",), 4 * k) for k in reversed(range(1, rest))]
     own_rows, = pack([[(0, 0, index_rows.shape[0])]], index_rows)
 
     bits = [loop // 2 >> i for i in range(loop.bit_length() - 4)] + [4, 2, 1]
@@ -268,7 +268,7 @@
     half_top = top // 2
     inner, outer = range(1, half_top + 1), range(half_top + 1, top)
     opposite_plane = over(plane)
-    middle_masks, late_masks = range(top + 1, chips, 2), range(top, chips, 2)
+    middle_masks, late_masks = range(chips - 1, top, -2), range(chips - 2, top - 1, -2)
     sends = dict(zip(range(top, chips), sends))
     middle = [send(m, sends[m]) for m in middle_masks]
     held_back = [sends[m] for m in late_masks]

time: 85.2 us -> 85.9 us (level)
  waiting for transfers between devices: 32 us -> 36.1 us
  starting transfers between devices: 36.6 us -> 33.1 us
    ppermute x27, waiting for transfers between devices: 32 us -> 36.1 us  [exchange(): return lax.ppermute(value, axes, [(i, i ^ mask) for i in range(size)])]
    ppermute x27, starting transfers between devices: 36.6 us -> 33.1 us  [exchange(): return lax.ppermute(value, axes, [(i, i ^ mask) for i in range(size)])]
  transfers between devices with their start and end apart: 27 -> 27, of which waited for: 12 -> 11; matrix products, arithmetic and copies ran while one was open for 1% -> 1% of each run, Pallas kernels for 6% -> 6%
where the time goes in v3:
time: 85.9 us; the launch traced here: 85.7 us
  waiting for transfers between devices  36.1 us (42%)
  starting transfers between devices  33.1 us (39%)
  Pallas kernels  9.59 us (11%)
  between operations  3.21 us (4%)
  local copies, waits for them, and re-layouts  2.88 us (3%)
    ppermute x27, waiting for transfers between devices, exchange(): return lax.ppermute(value, axes, [(i, i ^ mask) for i in range(size)])  36.1 us
    ppermute x27, starting transfers between devices, exchange(): return lax.ppermute(value, axes, [(i, i ^ mask) for i in range(size)])  33.1 us
    pallas_call x1, Pallas kernels, shards(): pl.pallas_call(grad_kernel, out_shape=[jax.ShapeDtypeStruct((count, width...  3.28 us
    pallas_call x1, Pallas kernels, shards(): pl.pallas_call(functools.partial(score_kernel, last_counts, len(other_pai...  2.45 us
    unnamed x12, local copies, waits for them, and re-layouts  2.29 us
  transfers between devices with their start and end apart: 27, of which 11 were waited for; matrix products, arithmetic and copies ran while one was open for 1% of the time, Pallas kernels for 6%

profile of v3, /device:TPU:0, one launch (start us, length us, event | category | flops | bytes accessed | tf_op | source)
XLA Modules:
  0.0 85.7 jit_solution(9838887748819845526)
XLA Ops:
  1.1 2.6 %collective-permute-start.2 = (s32[8,32]{1,0:T(8,128)}, s32[8,32]{1,0:T(8,128)S(1)}, u32[]{:S(2)}, u32[]{:S(2)}) collective-permute-start(s32[8,32]{1,0:T(8,128)} %bitcast.7), channel_id=1, source_target_pairs={{0,4},{2,6},{4,0},{6,2},{8,12},{10,14},{12,8},{14,10},{16,20},{18,... | collective-permute-start | bytes 3080 | tf_op jit(solution)/shard_map/ppermute | solution.py:25
  3.7 2.6 %collective-permute-start.1 = (bf16[8,4096]{1,0:T(8,128)(2,1)}, bf16[8,4096]{1,0:T(8,128)(2,1)S(1)}, u32[]{:S(2)}, u32[]{:S(2)}) collective-permute-start(bf16[8,4096]{1,0:T(8,128)(2,1)} %refs_0_.3), channel_id=1, source_target_pairs={{0,16},{2,18},{4,20},{6,22},{8,24},{10,26},{12,28},{14,30},{16,0},... | collective-permute-start | bytes 196616 | tf_op jit(solution)/shard_map/ppermute | solution.py:25
  7.0 2.6 %collective-permute-start.3 = (s32[16,32]{1,0:T(8,128)S(1)}, s32[16,32]{1,0:T(8,128)S(1)}, u32[]{:S(2)}, u32[]{:S(2)}) collective-permute-start(s32[16,32]{1,0:T(8,128)S(1)} %shard_map.87.refs_0_), channel_id=1, source_target_pairs={{0,24},{2,26},{4,28},{6,30},{8,16},{10,18},{12,20},{14,22},{16,8},... | collective-permute-start | bytes 6152 | tf_op jit(solution)/shard_map/ppermute | solution.py:25
  11.5 1.6 %copy-done.1 = bf16[256,4096]{1,0:T(8,128)(2,1)S(1)} copy-done((bf16[256,4096]{1,0:T(8,128)(2,1)S(1)}, bf16[256,4096]{1,0:T(8,128)(2,1)}, u32[]{:S(2)}) %copy-start.1) | copy-done | bytes 2097176
  14.2 1.4 %shard_map.88 = (bf16[64,4096]{1,0:T(8,128)(2,1)S(1)}, bf16[16,4096]{1,0:T(8,128)(2,1)S(1)}, bf16[16,4096]{1,0:T(8,128)(2,1)S(1)}, bf16[16,4096]{1,0:T(8,128)(2,1)S(1)}, bf16[16,4096]{1,0:T(8,128)(2,1)S(1)}) custom-call(s32[2]{0:T(128)S(1)} %pad_add_fusion.meta, bf16[256,4096]{1,0:T(8,128)(2,1)S(1)} %collective-permute-done.other, ...), custom_call_target="tpu_custom_call" | custom-call | flops 268435456 | bytes 6291456 | tf_op jit(solution)/shard_map/pallas_call | solution.py:244
  15.7 1.6 %collective-permute-start.6 = (bf16[64,4096]{1,0:T(8,128)(2,1)S(1)}, bf16[64,4096]{1,0:T(8,128)(2,1)S(1)}, u32[]{:S(2)}, u32[]{:S(2)}) collective-permute-start(bf16[64,4096]{1,0:T(8,128)(2,1)S(1)} %get-tuple-element.33.refs_0_.refs_2_), channel_id=1, source_target_pairs={{0,1},{1,0},{2,3},{3,2},{4,5},{5,4},{6,7},{7,6},{8,9},{9,8},{10,11... | collective-permute-start | bytes 1572872 | tf_op jit(solution)/shard_map/ppermute | solution.py:25
  18.2 3.5 %collective-permute-start.7 = (bf16[16,4096]{1,0:T(8,128)(2,1)S(1)}, bf16[16,4096]{1,0:T(8,128)(2,1)S(1)}, u32[]{:S(2)}, u32[]{:S(2)}) collective-permute-start(bf16[16,4096]{1,0:T(8,128)(2,1)S(1)} %get-tuple-element.34), channel_id=1, source_target_pairs={{0,28},{2,30},{4,24},{6,26},{8,20},{10,22},{12,16},{14,18},{16,12}... | collective-permute-start | bytes 393224 | tf_op jit(solution)/shard_map/ppermute | solution.py:25
  21.7 1.5 %collective-permute-done.9.refs_5_ = bf16[16,4096]{1,0:T(8,128)(2,1)S(1)} collective-permute-done((bf16[16,4096]{1,0:T(8,128)(2,1)S(1)}, bf16[16,4096]{1,0:T(8,128)(2,1)S(1)}, u32[]{:S(2)}, u32[]{:S(2)}) %collective-permute-start.9) | collective-permute-done | bytes 131104 | tf_op jit(solution)/shard_map/ppermute | solution.py:25
  23.2 3.9 %collective-permute-done.7.refs_2_ = bf16[16,4096]{1,0:T(8,128)(2,1)S(1)} collective-permute-done((bf16[16,4096]{1,0:T(8,128)(2,1)S(1)}, bf16[16,4096]{1,0:T(8,128)(2,1)S(1)}, u32[]{:S(2)}, u32[]{:S(2)}) %collective-permute-start.7) | collective-permute-done | bytes 131104 | tf_op jit(solution)/shard_map/ppermute | solution.py:25
  27.2 4.1 %collective-permute-done.8.refs_3_ = bf16[16,4096]{1,0:T(8,128)(2,1)S(1)} collective-permute-done((bf16[16,4096]{1,0:T(8,128)(2,1)S(1)}, bf16[16,4096]{1,0:T(8,128)(2,1)S(1)}, u32[]{:S(2)}, u32[]{:S(2)}) %collective-permute-start.8) | collective-permute-done | bytes 131104 | tf_op jit(solution)/shard_map/ppermute | solution.py:25
  33.0 2.7 %collective-permute-start.10 = (bf16[16,4096]{1,0:T(8,128)(2,1)S(1)}, bf16[16,4096]{1,0:T(8,128)(2,1)S(1)}, u32[]{:S(2)}, u32[]{:S(2)}) collective-permute-start(bf16[16,4096]{1,0:T(8,128)(2,1)S(1)} %get-tuple-element.39), channel_id=1, source_target_pairs={{0,24},{2,26},{4,28},{6,30},{8,16},{10,18},{12,20},{14,22},{16,8},... | collective-permute-start | bytes 393224 | tf_op jit(solution)/shard_map/ppermute | solution.py:25
  36.5 7.1 %collective-permute-done.10.refs_3_ = bf16[16,4096]{1,0:T(8,128)(2,1)S(1)} collective-permute-done((bf16[16,4096]{1,0:T(8,128)(2,1)S(1)}, bf16[16,4096]{1,0:T(8,128)(2,1)S(1)}, u32[]{:S(2)}, u32[]{:S(2)}) %collective-permute-start.10) | collective-permute-done | bytes 131104 | tf_op jit(solution)/shard_map/ppermute | solution.py:25
  43.6 2.9 %collective-permute-done.11.refs_4_ = bf16[16,4096]{1,0:T(8,128)(2,1)S(1)} collective-permute-done((bf16[16,4096]{1,0:T(8,128)(2,1)S(1)}, bf16[16,4096]{1,0:T(8,128)(2,1)S(1)}, u32[]{:S(2)}, u32[]{:S(2)}) %collective-permute-start.11) | collective-permute-done | bytes 131104 | tf_op jit(solution)/shard_map/ppermute | solution.py:25
  46.6 1.4 %collective-permute-start.16 = (bf16[32,4096]{1,0:T(8,128)(2,1)S(1)}, bf16[32,4096]{1,0:T(8,128)(2,1)S(1)}, u32[]{:S(2)}, u32[]{:S(2)}) collective-permute-start(bf16[32,4096]{1,0:T(8,128)(2,1)S(1)} %get-tuple-element.45.refs_8_), channel_id=1, source_target_pairs={{0,1},{1,0},{2,3},{3,2},{4,5},{5,4},{6,7},{7,6},{8,9},{9,8},{10,11... | collective-permute-start | bytes 786440 | tf_op jit(solution)/shard_map/ppermute | solution.py:25
  49.4 4.5 %collective-permute-done.15.refs_0_ = bf16[32,4096]{1,0:T(8,128)(2,1)S(1)} collective-permute-done((bf16[32,4096]{1,0:T(8,128)(2,1)S(1)}, bf16[32,4096]{1,0:T(8,128)(2,1)S(1)}, u32[]{:S(2)}, u32[]{:S(2)}) %collective-permute-start.15) | collective-permute-done | bytes 262176 | tf_op jit(solution)/shard_map/ppermute | solution.py:25
  53.9 2.4 %shard_map.93 = (bf16[256,256]{1,0:T(8,128)(2,1)S(1)}, bf16[256,128]{1,0:T(8,128)(2,1)S(1)}, bf16[128,4096]{1,0:T(8,128)(2,1)S(1)}, f32[64,4352]{1,0:T(8,128)S(1)}) custom-call(s32[2]{0:T(128)S(1)} %pad_add_fusion.meta, s32[1,32]{1,0:T(1,128)S(1)} %copy-done.5, bf16[256,4096]{1,0:T(8,128)(2,1)S(1)} %copy-done, s32[1,256]{1,0:T(1,128)S(1)} %bitcast.9, ...), custom_call_target="tpu_custom_call" | custom-call | flops 411041792 | bytes 5308416 | tf_op jit(solution)/shard_map/pallas_call | solution.py:340
  57.5 1.7 %collective-permute-done.19.sent = f32[64,4352]{1,0:T(8,128)S(1)} collective-permute-done((f32[64,4352]{1,0:T(8,128)S(1)}, f32[64,4352]{1,0:T(8,128)S(1)}, u32[]{:S(2)}, u32[]{:S(2)}) %collective-permute-start.19) | collective-permute-done | bytes 1114144 | tf_op jit(solution)/shard_map/ppermute | solution.py:25
  61.3 1.6 %collective-permute-start.22 = (bf16[32,2176]{1,0:T(8,128)(2,1)S(1)}, bf16[32,2176]{1,0:T(8,128)(2,1)S(1)}, u32[]{:S(2)}, u32[]{:S(2)}) collective-permute-start(bf16[32,2176]{1,0:T(8,128)(2,1)S(1)} %get-tuple-element.57), channel_id=1, source_target_pairs={{0,5},{1,4},{2,7},{3,6},{4,1},{5,0},{6,3},{7,2},{8,13},{9,12},{10,... | collective-permute-start | bytes 417800 | tf_op jit(solution)/shard_map/ppermute | solution.py:25
  62.9 3.3 %shard_map.94 = (f32[256,4096]{1,0:T(8,128)}, f32[8,128]{1,0:T(8,128)S(1)}) custom-call(bf16[256,256]{1,0:T(8,128)(2,1)S(1)} %get-tuple-element.48.weights_1.weights, bf16[256,128]{1,0:T(8,128)(2,1)S(1)} %get-tuple-element.49.weights_2, bf16[256,4096]{1,0:T(8,128)(2,1)S(1)} %get-tuple-element.50.rows_1, bf16[128,4096]{1,0:T(8,128)(2,1)S(1)} %get-tuple-element.51.rows_2), custom_call_target="tpu_custom_call" | custom-call | flops 805306368 | bytes 7340032 | tf_op jit(solution)/shard_map/pallas_call | solution.py:372
  66.2 5.7 %collective-permute-done.22.from_xy = bf16[32,2176]{1,0:T(8,128)(2,1)S(1)} collective-permute-done((bf16[32,2176]{1,0:T(8,128)(2,1)S(1)}, bf16[32,2176]{1,0:T(8,128)(2,1)S(1)}, u32[]{:S(2)}, u32[]{:S(2)}) %collective-permute-start.22) | collective-permute-done | bytes 139296 | tf_op jit(solution)/shard_map/ppermute | solution.py:25
  72.0 2.0 %collective-permute-start.23 = (f32[8,2176]{1,0:T(8,128)S(1)}, f32[8,2176]{1,0:T(8,128)S(1)}, u32[]{:S(2)}, u32[]{:S(2)}) collective-permute-start(f32[8,2176]{1,0:T(8,128)S(1)} %get-tuple-element.60), channel_id=1, source_target_pairs={{0,24},{2,26},{4,28},{6,30},{8,16},{10,18},{12,20},{14,22},{16,8},... | collective-permute-start | bytes 208904 | tf_op jit(solution)/shard_map/ppermute | solution.py:25
  74.7 1.8 %collective-permute-start.25 = (bf16[8,2176]{1,0:T(8,128)(2,1)S(1)}, bf16[8,2176]{1,0:T(8,128)(2,1)S(1)}, u32[]{:S(2)}, u32[]{:S(2)}) collective-permute-start(bf16[8,2176]{1,0:T(8,128)(2,1)S(1)} %get-tuple-element.62), channel_id=1, source_target_pairs={{0,16},{2,18},{4,20},{6,22},{8,24},{10,26},{12,28},{14,30},{16,0},... | collective-permute-start | bytes 104456 | tf_op jit(solution)/shard_map/ppermute | solution.py:25
  76.5 3.0 %collective-permute-done.25 = bf16[8,2176]{1,0:T(8,128)(2,1)S(1)} collective-permute-done((bf16[8,2176]{1,0:T(8,128)(2,1)S(1)}, bf16[8,2176]{1,0:T(8,128)(2,1)S(1)}, u32[]{:S(2)}, u32[]{:S(2)}) %collective-permute-start.25) | collective-permute-done | bytes 34848 | tf_op jit(solution)/shard_map/ppermute | solution.py:25
  79.6 1.7 %collective-permute-start.26 = (f32[8,2048]{1,0:T(8,128)S(1)}, f32[8,2048]{1,0:T(8,128)S(1)}, u32[]{:S(2)}, u32[]{:S(2)}) collective-permute-start(f32[8,2048]{1,0:T(8,128)S(1)} %slice.12), channel_id=1, source_target_pairs={{0,1},{1,0},{2,3},{3,2},{4,5},{5,4},{6,7},{7,6},{8,9},{9,8},{10,11... | collective-permute-start | bytes 196616 | tf_op jit(solution)/shard_map/ppermute | solution.py:25
  (60 shorter events, 15.1 us)
Async XLA Ops:
  0.6 13.6 %collective-permute-start = (bf16[256,4096]{1,0:T(8,128)(2,1)}, bf16[256,4096]{1,0:T(8,128)(2,1)S(1)}, u32[]{:S(2)}, u32[]{:S(2)}) collective-permute-start(bf16[256,4096]{1,0:T(8,128)(2,1)} %refs_0_.2), channel_id=1, source_target_pairs={{0,2},{2,0},{4,6},{6,4},{8,10},{10,8},{12,14},{14,12},{16,18},{18,... | collective-permute-start | bytes 6291464 | tf_op jit(solution)/shard_map/ppermute | solution.py:25
  1.1 5.8 %collective-permute-start.2 = (s32[8,32]{1,0:T(8,128)}, s32[8,32]{1,0:T(8,128)S(1)}, u32[]{:S(2)}, u32[]{:S(2)}) collective-permute-start(s32[8,32]{1,0:T(8,128)} %bitcast.7), channel_id=1, source_target_pairs={{0,4},{2,6},{4,0},{6,2},{8,12},{10,14},{12,8},{14,10},{16,20},{18,... | collective-permute-start | bytes 3080 | tf_op jit(solution)/shard_map/ppermute | solution.py:25
  3.7 10.5 %collective-permute-start.1 = (bf16[8,4096]{1,0:T(8,128)(2,1)}, bf16[8,4096]{1,0:T(8,128)(2,1)S(1)}, u32[]{:S(2)}, u32[]{:S(2)}) collective-permute-start(bf16[8,4096]{1,0:T(8,128)(2,1)} %refs_0_.3), channel_id=1, source_target_pairs={{0,16},{2,18},{4,20},{6,22},{8,24},{10,26},{12,28},{14,30},{16,0},... | collective-permute-start | bytes 196616 | tf_op jit(solution)/shard_map/ppermute | solution.py:25
  7.0 6.3 %collective-permute-start.3 = (s32[16,32]{1,0:T(8,128)S(1)}, s32[16,32]{1,0:T(8,128)S(1)}, u32[]{:S(2)}, u32[]{:S(2)}) collective-permute-start(s32[16,32]{1,0:T(8,128)S(1)} %shard_map.87.refs_0_), channel_id=1, source_target_pairs={{0,24},{2,26},{4,28},{6,30},{8,16},{10,18},{12,20},{14,22},{16,8},... | collective-permute-start | bytes 6152 | tf_op jit(solution)/shard_map/ppermute | solution.py:25
  9.6 4.5 %collective-permute-start.4 = (s32[16,32]{1,0:T(8,128)S(1)}, s32[16,32]{1,0:T(8,128)S(1)}, u32[]{:S(2)}, u32[]{:S(2)}) collective-permute-start(s32[16,32]{1,0:T(8,128)S(1)} %shard_map.87.refs_0_), channel_id=1, source_target_pairs={{0,16},{2,18},{4,20},{6,22},{8,24},{10,26},{12,28},{14,30},{16,0},... | collective-permute-start | bytes 6152 | tf_op jit(solution)/shard_map/ppermute | solution.py:25
  15.7 15.6 %collective-permute-start.6 = (bf16[64,4096]{1,0:T(8,128)(2,1)S(1)}, bf16[64,4096]{1,0:T(8,128)(2,1)S(1)}, u32[]{:S(2)}, u32[]{:S(2)}) collective-permute-start(bf16[64,4096]{1,0:T(8,128)(2,1)S(1)} %get-tuple-element.33.refs_0_.refs_2_), channel_id=1, source_target_pairs={{0,1},{1,0},{2,3},{3,2},{4,5},{5,4},{6,7},{7,6},{8,9},{9,8},{10,11... | collective-permute-start | bytes 1572872 | tf_op jit(solution)/shard_map/ppermute | solution.py:25
  17.3 6.0 %collective-permute-start.9 = (bf16[16,4096]{1,0:T(8,128)(2,1)S(1)}, bf16[16,4096]{1,0:T(8,128)(2,1)S(1)}, u32[]{:S(2)}, u32[]{:S(2)}) collective-permute-start(bf16[16,4096]{1,0:T(8,128)(2,1)S(1)} %shard_map.89.refs_4_), channel_id=1, source_target_pairs={{0,8},{2,10},{4,12},{6,14},{8,0},{10,2},{12,4},{14,6},{16,24},{18,... | collective-permute-start | bytes 393224 | tf_op jit(solution)/shard_map/ppermute | solution.py:25
  18.2 8.9 %collective-permute-start.7 = (bf16[16,4096]{1,0:T(8,128)(2,1)S(1)}, bf16[16,4096]{1,0:T(8,128)(2,1)S(1)}, u32[]{:S(2)}, u32[]{:S(2)}) collective-permute-start(bf16[16,4096]{1,0:T(8,128)(2,1)S(1)} %get-tuple-element.34), channel_id=1, source_target_pairs={{0,28},{2,30},{4,24},{6,26},{8,20},{10,22},{12,16},{14,18},{16,12}... | collective-permute-start | bytes 393224 | tf_op jit(solution)/shard_map/ppermute | solution.py:25
  21.7 9.5 %collective-permute-start.8 = (bf16[16,4096]{1,0:T(8,128)(2,1)S(1)}, bf16[16,4096]{1,0:T(8,128)(2,1)S(1)}, u32[]{:S(2)}, u32[]{:S(2)}) collective-permute-start(bf16[16,4096]{1,0:T(8,128)(2,1)S(1)} %get-tuple-element.35), channel_id=1, source_target_pairs={{0,20},{2,22},{4,16},{6,18},{8,28},{10,30},{12,24},{14,26},{16,4},... | collective-permute-start | bytes 393224 | tf_op jit(solution)/shard_map/ppermute | solution.py:25
  31.4 15.1 %collective-permute-start.12 = (bf16[64,4096]{1,0:T(8,128)(2,1)S(1)}, bf16[64,4096]{1,0:T(8,128)(2,1)S(1)}, u32[]{:S(2)}, u32[]{:S(2)}) collective-permute-start(bf16[64,4096]{1,0:T(8,128)(2,1)S(1)} %get-tuple-element.38.refs_2_), channel_id=1, source_target_pairs={{0,4},{2,6},{4,0},{6,2},{8,12},{10,14},{12,8},{14,10},{16,20},{18,... | collective-permute-start | bytes 1572872 | tf_op jit(solution)/shard_map/ppermute | solution.py:25
  32.5 14.0 %collective-permute-start.13 = (bf16[32,4096]{1,0:T(8,128)(2,1)S(1)}, bf16[32,4096]{1,0:T(8,128)(2,1)S(1)}, u32[]{:S(2)}, u32[]{:S(2)}) collective-permute-start(bf16[32,4096]{1,0:T(8,128)(2,1)S(1)} %get-tuple-element.41), channel_id=1, source_target_pairs={{0,8},{2,10},{4,12},{6,14},{8,0},{10,2},{12,4},{14,6},{16,24},{18,... | collective-permute-start | bytes 786440 | tf_op jit(solution)/shard_map/ppermute | solution.py:25
  32.5 14.0 %collective-permute-start.14 = (bf16[32,4096]{1,0:T(8,128)(2,1)S(1)}, bf16[32,4096]{1,0:T(8,128)(2,1)S(1)}, u32[]{:S(2)}, u32[]{:S(2)}) collective-permute-start(bf16[32,4096]{1,0:T(8,128)(2,1)S(1)} %get-tuple-element.42.refs_6_), channel_id=1, source_target_pairs={{0,1},{1,0},{2,3},{3,2},{4,5},{5,4},{6,7},{7,6},{8,9},{9,8},{10,11... | collective-permute-start | bytes 786440 | tf_op jit(solution)/shard_map/ppermute | solution.py:25
  33.0 10.6 %collective-permute-start.10 = (bf16[16,4096]{1,0:T(8,128)(2,1)S(1)}, bf16[16,4096]{1,0:T(8,128)(2,1)S(1)}, u32[]{:S(2)}, u32[]{:S(2)}) collective-permute-start(bf16[16,4096]{1,0:T(8,128)(2,1)S(1)} %get-tuple-element.39), channel_id=1, source_target_pairs={{0,24},{2,26},{4,28},{6,30},{8,16},{10,18},{12,20},{14,22},{16,8},... | collective-permute-start | bytes 393224 | tf_op jit(solution)/shard_map/ppermute | solution.py:25
  35.7 10.8 %collective-permute-start.11 = (bf16[16,4096]{1,0:T(8,128)(2,1)S(1)}, bf16[16,4096]{1,0:T(8,128)(2,1)S(1)}, u32[]{:S(2)}, u32[]{:S(2)}) collective-permute-start(bf16[16,4096]{1,0:T(8,128)(2,1)S(1)} %get-tuple-element.40), channel_id=1, source_target_pairs={{0,16},{2,18},{4,20},{6,22},{8,24},{10,26},{12,28},{14,30},{16,0},... | collective-permute-start | bytes 393224 | tf_op jit(solution)/shard_map/ppermute | solution.py:25
  46.6 7.3 %collective-permute-start.15 = (bf16[32,4096]{1,0:T(8,128)(2,1)S(1)}, bf16[32,4096]{1,0:T(8,128)(2,1)S(1)}, u32[]{:S(2)}, u32[]{:S(2)}) collective-permute-start(bf16[32,4096]{1,0:T(8,128)(2,1)S(1)} %get-tuple-element.47), channel_id=1, source_target_pairs={{0,12},{2,14},{4,8},{6,10},{8,4},{10,6},{12,0},{14,2},{16,28},{18,... | collective-permute-start | bytes 786440 | tf_op jit(solution)/shard_map/ppermute | solution.py:25
  46.6 7.3 %collective-permute-start.16 = (bf16[32,4096]{1,0:T(8,128)(2,1)S(1)}, bf16[32,4096]{1,0:T(8,128)(2,1)S(1)}, u32[]{:S(2)}, u32[]{:S(2)}) collective-permute-start(bf16[32,4096]{1,0:T(8,128)(2,1)S(1)} %get-tuple-element.45.refs_8_), channel_id=1, source_target_pairs={{0,1},{1,0},{2,3},{3,2},{4,5},{5,4},{6,7},{7,6},{8,9},{9,8},{10,11... | collective-permute-start | bytes 786440 | tf_op jit(solution)/shard_map/ppermute | solution.py:25
  48.1 5.8 %collective-permute-start.17 = (bf16[32,4096]{1,0:T(8,128)(2,1)S(1)}, bf16[32,4096]{1,0:T(8,128)(2,1)S(1)}, u32[]{:S(2)}, u32[]{:S(2)}) collective-permute-start(bf16[32,4096]{1,0:T(8,128)(2,1)S(1)} %get-tuple-element.43.refs_0_), channel_id=1, source_target_pairs={{0,2},{2,0},{4,6},{6,4},{8,10},{10,8},{12,14},{14,12},{16,18},{18,... | collective-permute-start | bytes 786440 | tf_op jit(solution)/shard_map/ppermute | solution.py:25
  48.1 5.8 %collective-permute-start.18 = (bf16[32,4096]{1,0:T(8,128)(2,1)S(1)}, bf16[32,4096]{1,0:T(8,128)(2,1)S(1)}, u32[]{:S(2)}, u32[]{:S(2)}) collective-permute-start(bf16[32,4096]{1,0:T(8,128)(2,1)S(1)} %get-tuple-element.44.refs_1_), channel_id=1, source_target_pairs={{0,2},{2,0},{4,6},{6,4},{8,10},{10,8},{12,14},{14,12},{16,18},{18,... | collective-permute-start | bytes 786440 | tf_op jit(solution)/shard_map/ppermute | solution.py:25
  59.3 12.6 %collective-permute-start.20 = (f32[32,2176]{1,0:T(8,128)S(1)}, f32[32,2176]{1,0:T(8,128)S(1)}, u32[]{:S(2)}, u32[]{:S(2)}) collective-permute-start(f32[32,2176]{1,0:T(8,128)S(1)} %get-tuple-element.55), channel_id=1, source_target_pairs={{0,4},{1,5},{2,6},{3,7},{4,0},{5,1},{6,2},{7,3},{8,12},{9,13},{10,... | collective-permute-start | bytes 835592 | tf_op jit(solution)/shard_map/ppermute | solution.py:25
  59.9 12.0 %collective-permute-start.21 = (f32[32,2176]{1,0:T(8,128)S(1)}, f32[32,2176]{1,0:T(8,128)S(1)}, u32[]{:S(2)}, u32[]{:S(2)}) collective-permute-start(f32[32,2176]{1,0:T(8,128)S(1)} %get-tuple-element.56), channel_id=1, source_target_pairs={{0,1},{1,0},{2,3},{3,2},{4,5},{5,4},{6,7},{7,6},{8,9},{9,8},{10,11... | collective-permute-start | bytes 835592 | tf_op jit(solution)/shard_map/ppermute | solution.py:25
  61.3 10.6 %collective-permute-start.22 = (bf16[32,2176]{1,0:T(8,128)(2,1)S(1)}, bf16[32,2176]{1,0:T(8,128)(2,1)S(1)}, u32[]{:S(2)}, u32[]{:S(2)}) collective-permute-start(bf16[32,2176]{1,0:T(8,128)(2,1)S(1)} %get-tuple-element.57), channel_id=1, source_target_pairs={{0,5},{1,4},{2,7},{3,6},{4,1},{5,0},{6,3},{7,2},{8,13},{9,12},{10,... | collective-permute-start | bytes 417800 | tf_op jit(solution)/shard_map/ppermute | solution.py:25
  72.0 7.5 %collective-permute-start.23 = (f32[8,2176]{1,0:T(8,128)S(1)}, f32[8,2176]{1,0:T(8,128)S(1)}, u32[]{:S(2)}, u32[]{:S(2)}) collective-permute-start(f32[8,2176]{1,0:T(8,128)S(1)} %get-tuple-element.60), channel_id=1, source_target_pairs={{0,24},{2,26},{4,28},{6,30},{8,16},{10,18},{12,20},{14,22},{16,8},... | collective-permute-start | bytes 208904 | tf_op jit(solution)/shard_map/ppermute | solution.py:25
  74.0 5.5 %collective-permute-start.24 = (f32[8,2176]{1,0:T(8,128)S(1)}, f32[8,2176]{1,0:T(8,128)S(1)}, u32[]{:S(2)}, u32[]{:S(2)}) collective-permute-start(f32[8,2176]{1,0:T(8,128)S(1)} %get-tuple-element.61), channel_id=1, source_target_pairs={{0,8},{2,10},{4,12},{6,14},{8,0},{10,2},{12,4},{14,6},{16,24},{18,... | collective-permute-start | bytes 208904 | tf_op jit(solution)/shard_map/ppermute | solution.py:25
  74.7 4.8 %collective-permute-start.25 = (bf16[8,2176]{1,0:T(8,128)(2,1)S(1)}, bf16[8,2176]{1,0:T(8,128)(2,1)S(1)}, u32[]{:S(2)}, u32[]{:S(2)}) collective-permute-start(bf16[8,2176]{1,0:T(8,128)(2,1)S(1)} %get-tuple-element.62), channel_id=1, source_target_pairs={{0,16},{2,18},{4,20},{6,22},{8,24},{10,26},{12,28},{14,30},{16,0},... | collective-permute-start | bytes 104456 | tf_op jit(solution)/shard_map/ppermute | solution.py:25
  (9 other events, 46.5 us)
